TPU v7x, 32 devices: a whole 2x2x4 slice. The times are simulated.
32 devices in a mesh: seq: 16 (over z, y, core), head: 2 (over x).
Axes of the slice: x: 2, y: 2, z: 4, core: 2. Of those that a mesh axis runs over, the one named last changes fastest.
Arguments:
- inputs: bfloat16 [8192, 5376], P('seq'), may hold values from -6 to 6
- queries: bfloat16 [8192, 4096], P('seq', 'head'), may hold values from -6 to 6
- key_matrix: bfloat16 [5376, 2048], P('seq', 'head'), may hold values from -0.078125 to 0.078125
- value_matrix: bfloat16 [5376, 2048], P('seq', 'head'), may hold values from -0.078125 to 0.078125
- readout: bfloat16 [4096, 512], P('head'), may hold values from -6 to 6
- token_mask: int32 [8192], P('seq'), may hold values 0 or 1
- targets: int32 [8192], P('seq'), may hold values from 0 to 511
Outputs:
- query_grad: float32 [8192, 4096], P('seq', 'head')
- input_grad: float32 [8192, 5376], P('seq', 'head')
All inputs are finite; a program needn't handle non-finite values. No bound on the sum of `token_mask` on one device may be relied on, other than what follows from the above.
Results may differ from a plain program's by a relative error of at most 0.028.
Values may be sent and summed in bfloat16 or wider, within the bound.
A program may use at most 256 MiB of HBM per device.

v0:
```python
import jax
import jax.numpy as jnp
from jax import lax
from jax.sharding import PartitionSpec as P

HEAD_SIZE = 128
WINDOW_KEYS = 1024


norm_eps = 1e-06
softcap = 30.0
score_scale = 168.0 ** (-0.5)


def passed_along(value, axis, steps):
    count = lax.axis_size(axis)
    leading, last = (max(0, -steps), min(count, count - steps))
    return lax.ppermute(value, axis, [(source, source + steps) for source in range(leading, last)])


def normalized_rows(value_rows):
    inverse = lax.rsqrt(jnp.mean(value_rows * value_rows, axis=-1, keepdims=True) + norm_eps)
    return (value_rows * inverse, inverse)


def unit_norm_backward(unit, inverse, upstream):
    return inverse * (upstream - unit * jnp.mean(unit * upstream, axis=-1, keepdims=True))


def shards(inputs, queries, key_matrix, value_matrix, readout, token_mask, targets):
    tokens = inputs.shape[0]
    kv_width = key_matrix.shape[1]
    kv_heads = kv_width // HEAD_SIZE
    q_heads = queries.shape[1] // HEAD_SIZE
    query_groups = q_heads // kv_heads
    reach = WINDOW_KEYS // tokens
    span = (reach + 1) * tokens
    stacked = jnp.concatenate([key_matrix, value_matrix], axis=1)
    full_weight = lax.all_gather(stacked, "seq", axis=0, tiled=True)
    projected = jnp.dot(inputs, full_weight, preferred_element_type=jnp.float32)
    key_unscaled = projected[:, :kv_width].reshape(tokens, kv_heads, HEAD_SIZE)
    value_rows = projected[:, kv_width:].astype(jnp.bfloat16).reshape(tokens, kv_heads, HEAD_SIZE)
    key_unit_rows, key_inverse_norm = normalized_rows(key_unscaled)
    key_normalized_rows = key_unit_rows.astype(jnp.bfloat16)
    query_unit_rows, query_inverse_norm = normalized_rows(
        queries.astype(jnp.float32).reshape(tokens, kv_heads, query_groups, HEAD_SIZE)
    )
    query_hat = query_unit_rows.astype(jnp.bfloat16)
    paired = jnp.concatenate([key_normalized_rows, value_rows], axis=-1)
    moving = paired
    arrived = []
    for offset in range(reach):
        moving = passed_along(moving, "seq", 1)
        arrived.append(moving)
    earlier = arrived[::-1]
    window_kv = jnp.concatenate(earlier + [paired], axis=0)
    key_block = window_kv[..., :HEAD_SIZE]
    value_block = window_kv[..., HEAD_SIZE:]
    first = lax.axis_index("seq") * tokens
    query_pos = first + jnp.arange(tokens, dtype=jnp.int32)
    key_pos = first - reach * tokens + jnp.arange(span, dtype=jnp.int32)
    distance = query_pos[:, None] - key_pos[None, :]
    visible = (distance >= 0) & (distance < WINDOW_KEYS) & (key_pos[None, :] >= 0)
    scores = (
        jnp.einsum("qkgd,jkd->kgqj", query_hat, key_block, preferred_element_type=jnp.float32)
        * score_scale
    )
    raised = jnp.where(visible, jnp.exp(scores), 0.0)
    attn = (raised / jnp.sum(raised, axis=-1, keepdims=True)).astype(jnp.bfloat16)
    attended = jnp.einsum(
        "kgqj,jkd->qkgd", attn, value_block, preferred_element_type=jnp.float32
    ).astype(jnp.bfloat16)
    flat = attended.reshape(tokens, q_heads * HEAD_SIZE)
    partial_value = jnp.dot(flat, readout, preferred_element_type=jnp.float32)
    logits = lax.psum(partial_value.astype(jnp.bfloat16), "head").astype(jnp.float32)
    capped = softcap * jnp.tanh(logits / softcap)
    expo = jnp.exp(capped)
    probs = expo / jnp.sum(expo, axis=-1, keepdims=True)
    onehot = (targets[:, None] == jnp.arange(logits.shape[1], dtype=jnp.int32)[None, :]).astype(
        jnp.float32
    )
    chosen = token_mask.astype(jnp.float32)[:, None]
    dlogits = (chosen * (probs - onehot) * (1.0 - (capped / softcap) ** 2)).astype(jnp.bfloat16)
    attended_grad = lax.dot_general(
        dlogits, readout, (((1,), (1,)), ((), ())), preferred_element_type=jnp.float32
    )
    attended_grad = attended_grad.astype(jnp.bfloat16).reshape(
        tokens, kv_heads, query_groups, HEAD_SIZE
    )
    d_weights = jnp.einsum(
        "qkgd,jkd->kgqj", attended_grad, value_block, preferred_element_type=jnp.float32
    )
    attn_f = attn.astype(jnp.float32)
    d_scores = (attn_f * (d_weights - jnp.sum(attn_f * d_weights, axis=-1, keepdims=True))).astype(
        jnp.bfloat16
    )
    d_query_hat = (
        jnp.einsum("kgqj,jkd->qkgd", d_scores, key_block, preferred_element_type=jnp.float32)
        * score_scale
    )
    d_key_hat = (
        jnp.einsum("kgqj,qkgd->jkd", d_scores, query_hat, preferred_element_type=jnp.float32)
        * score_scale
    )
    d_value = jnp.einsum("kgqj,qkgd->jkd", attn, attended_grad, preferred_element_type=jnp.float32)
    query_grad = unit_norm_backward(query_unit_rows, query_inverse_norm, d_query_hat).reshape(
        tokens, q_heads * HEAD_SIZE
    )
    pieces_all = jnp.concatenate([d_key_hat, d_value], axis=-1)
    pieces = [
        pieces_all[slot_index * tokens : (slot_index + 1) * tokens]
        for slot_index in range(reach + 1)
    ]
    total = pieces[0]
    for slot_index in range(1, reach + 1):
        total = (
            passed_along(total.astype(jnp.bfloat16), "seq", -1).astype(total.dtype)
            + pieces[slot_index]
        )
    key_weight_gradient = (
        unit_norm_backward(key_unit_rows, key_inverse_norm, total[..., :HEAD_SIZE])
        .astype(jnp.bfloat16)
        .reshape(tokens, kv_width)
    )
    value_weight_gradient = total[..., HEAD_SIZE:].astype(jnp.bfloat16).reshape(tokens, kv_width)
    both_grad = jnp.concatenate([key_weight_gradient, value_weight_gradient], axis=1)
    partial_grad = lax.dot_general(
        both_grad, full_weight, (((1,), (1,)), ((), ())), preferred_element_type=jnp.float32
    )
    input_grad = lax.psum_scatter(
        partial_grad.astype(jnp.bfloat16), "head", scatter_dimension=1, tiled=True
    ).astype(jnp.float32)
    return (query_grad, input_grad)


def solution(mesh):
    in_specs = (
        P("seq", None),
        P("seq", "head"),
        P("seq", "head"),
        P("seq", "head"),
        P("head", None),
        P("seq"),
        P("seq"),
    )
    out_specs = (P("seq", "head"), P("seq", "head"))
    return jax.shard_map(shards, mesh=mesh, in_specs=in_specs, out_specs=out_specs, check_vma=False)
```

profile of v0, /device:TPU:13, one launch (start us, length us, event | category | flops | bytes accessed | tf_op | source)
XLA Modules:
  0.0 585.5 jit_solution(2186064417357587457)
XLA Ops:
  10.0 115.3 %all-gather.2.cloned.1.call-done = bf16[5376,2048]{1,0:T(8,128)(2,1)} async-done(((bf16[336,2048]{1,0:T(8,128)(2,1)}), bf16[5376,2048]{1,0:T(8,128)(2,1)}) %all-gather.2.cloned.1.call-update) | async-done | bytes 22020112 | tf_op jit(solution)/shard_map/all_gather | solution.py:39
  125.3 16.5 %convolution_bitcast_fusion.1 = f32[512,2048]{0,1:T(8,128)S(1)} fusion(bf16[5376,2048]{1,0:T(8,128)(2,1)} %all-gather.2.cloned.1.call-done, bf16[512,5376]{1,0:T(8,128)(2,1)} %param.7), kind=kOutput, calls=%fused_computation.32 | convolution fusion | flops 11274289152 | bytes 31719424 | tf_op jit(solution)/shard_map/dot_general | solution.py:40
  154.8 23.0 %collective-permute-done = bf16[512,8,256]{2,0,1:T(8,128)(2,1)} collective-permute-done((bf16[512,8,256]{2,0,1:T(8,128)(2,1)S(1)}, bf16[512,8,256]{2,0,1:T(8,128)(2,1)}, u32[]{:S(2)}, u32[]{:S(2)}) %collective-permute-start) | collective-permute-done | bytes 2097184 | tf_op jit(solution)/shard_map/ppermute | solution.py:18
  177.8 5.9 %collective-permute-start.1 = (bf16[512,8,256]{2,0,1:T(8,128)(2,1)}, bf16[512,8,256]{2,0,1:T(8,128)(2,1)}, u32[]{:S(2)}, u32[]{:S(2)}) collective-permute-start(bf16[512,8,256]{2,0,1:T(8,128)(2,1)} %collective-permute-done), channel_id=1, source_target_pairs={{0,2},{2,4},{4,6},{6,8},{8,10},{10,12},{12,14},{14,16},{16,18},{18... | collective-permute-start | bytes 6291464 | tf_op jit(solution)/shard_map/ppermute | solution.py:18
  192.0 14.4 %collective-permute-done.1 = bf16[512,8,256]{2,0,1:T(8,128)(2,1)} collective-permute-done((bf16[512,8,256]{2,0,1:T(8,128)(2,1)}, bf16[512,8,256]{2,0,1:T(8,128)(2,1)}, u32[]{:S(2)}, u32[]{:S(2)}) %collective-permute-start.1) | collective-permute-done | bytes 2097184 | tf_op jit(solution)/shard_map/ppermute | solution.py:18
  206.5 5.3 maximum_maximum_fusion
  211.8 20.7 %fusion.2 = (f32[8,2,512]{2,1,0:T(2,128)S(1)}, f32[8,1536,512,2]{2,1,3,0:T(8,128)}) fusion(pred[512,1536]{0,1:T(8,128)(4,1)S(1)} %fusion.13, f32[512,2048]{0,1:T(8,128)S(1)} %copy-done.2, f32[512,8,2]{0,2,1:T(2,128)S(1)} %add_rsqrt_fusion, bf16[1536,8,256]{2,0,1:T(8,128)(2,1)} %maximum_maximum_fusion), kind=kOutput, calls=%fused_computation.7 | convolution fusion | flops 3261063168 | bytes 58523648 | tf_op jit(solution)/shard_map/qkgd,jkd->kgqj/dot_general | solution.py:65
  232.5 26.0 %divide_convert_fusion = bf16[8,2,512,1536]{2,3,1,0:T(8,128)(2,1)} fusion(f32[8,1536,512,2]{2,1,3,0:T(8,128)} %get-tuple-element.9, f32[8,2,512]{2,1,0:T(2,128)S(1)} %get-tuple-element.8, pred[512,1536]{0,1:T(8,128)(4,1)} %copy-done.6), kind=kLoop, calls=%fused_computation.6 | loop fusion | flops 50331648 | bytes 76316672 | tf_op jit(solution)/shard_map/convert_element_type | solution.py:69
  258.4 12.8 %fusion.21 = bf16[8,128,2,512]{3,1,2,0:T(8,128)(2,1)S(1)} fusion(bf16[8,2,512,1536]{2,3,1,0:T(8,128)(2,1)} %divide_convert_fusion, bf16[1536,8,256]{2,0,1:T(8,128)(2,1)} %maximum_maximum_fusion), kind=kOutput, calls=%fused_computation.51 | convolution fusion | flops 3222274048 | bytes 30408704 | tf_op jit(solution)/shard_map/kgqj,jkd->qkgd/dot_general | solution.py:70
  273.6 30.1 %all-reduce.2.cloned.1.call-done = bf16[512,512]{1,0:T(8,128)(2,1)} async-done(((bf16[512,512]{1,0:T(8,128)(2,1)}), bf16[512,512]{1,0:T(8,128)(2,1)}) %all-reduce.2.cloned.1.call-update) | async-done | bytes 524304 | tf_op jit(solution)/shard_map/psum | solution.py:75
  312.0 14.3 %convolution_bitcast_fusion = f32[1536,8,128]{2,0,1:T(8,128)} fusion(bf16[512,8,2,128]{0,3,2,1:T(8,128)(2,1)S(1)} %bitcast.94, bf16[8,2,512,1536]{2,3,1,0:T(8,128)(2,1)} %divide_convert_fusion), kind=kOutput, calls=%fused_computation.18 | convolution fusion | flops 3221225472 | bytes 33554432 | tf_op jit(solution)/shard_map/kgqj,qkgd->jkd/dot_general | solution.py:105
  326.3 26.3 %fusion = (f32[8,2,512]{2,1,0:T(2,128)S(1)}, f32[8,1536,512,2]{2,1,3,0:T(8,128)}) fusion(bf16[8,2,512,1536]{2,3,1,0:T(8,128)(2,1)} %divide_convert_fusion, bf16[512,8,2,128]{0,3,2,1:T(8,128)(2,1)S(1)} %bitcast.95, bf16[1536,8,256]{2,0,1:T(8,128)(2,1)} %maximum_maximum_fusion), kind=kOutput, calls=%fused_computation.2 | convolution fusion | flops 3258966016 | bytes 80773120 | tf_op jit(solution)/shard_map/qkgd,jkd->kgqj/dot_general | solution.py:90
  352.6 40.6 %fusion.1 = bf16[8,2,512,1536]{2,3,1,0:T(8,128)(2,1)} fusion(f32[8,1536,512,2]{2,1,3,0:T(8,128)} %get-tuple-element.11, f32[8,2,512]{2,1,0:T(2,128)S(1)} %get-tuple-element.10, f32[8,2,512]{2,1,0:T(2,128)S(1)} %get-tuple-element.8, f32[8,1536,512,2]{2,1,3,0:T(8,128)} %get-tuple-element.9, pred[512,1536]{0,1:T(8,128)(4,1)S(1)} %copy-done.7), kind=kLoop, calls=%fused_computation.3 | loop fusion | flops 100663296 | bytes 126681088 | tf_op jit(solution)/shard_map/convert_element_type | solution.py:94
  393.2 14.5 %fusion.3 = f32[1536,8,128]{2,0,1:T(8,128)} fusion(bf16[8,2,512,1536]{2,3,1,0:T(8,128)(2,1)} %fusion.1, f32[512,2048]{0,1:T(8,128)} %copy.41, f32[512,8,2]{0,2,1:T(2,128)S(1)} %add_rsqrt_fusion), kind=kOutput, calls=%fused_computation.15 | convolution fusion | flops 3224895488 | bytes 35684352 | tf_op jit(solution)/shard_map/kgqj,qkgd->jkd/dot_general | solution.py:102
  413.3 25.5 %collective-permute-done.2 = bf16[512,8,256]{2,0,1:T(8,128)(2,1)S(1)} collective-permute-done((bf16[512,8,256]{2,0,1:T(8,128)(2,1)S(1)}, bf16[512,8,256]{2,0,1:T(8,128)(2,1)S(1)}, u32[]{:S(2)}, u32[]{:S(2)}) %collective-permute-start.2) | collective-permute-done | bytes 2097184 | tf_op jit(solution)/shard_map/ppermute | solution.py:18
  443.3 26.1 %collective-permute-done.3 = bf16[512,8,256]{2,0,1:T(8,128)(2,1)S(1)} collective-permute-done((bf16[512,8,256]{2,0,1:T(8,128)(2,1)S(1)}, bf16[512,8,256]{2,0,1:T(8,128)(2,1)S(1)}, u32[]{:S(2)}, u32[]{:S(2)}) %collective-permute-start.3) | collective-permute-done | bytes 2097184 | tf_op jit(solution)/shard_map/ppermute | solution.py:18
  475.7 18.0 %convolution_convert_fusion = bf16[512,5376]{1,0:T(8,128)(2,1)} fusion(bf16[5376,2048]{1,0:T(8,128)(2,1)} %all-gather.2.cloned.1.call-done, bf16[512,1024]{0,1:T(8,128)(2,1)S(1)} %bitcast.101, bf16[512,1024]{0,1:T(8,128)(2,1)S(1)} %bitcast.102), kind=kOutput, calls=%fused_computation.12 | convolution fusion | flops 11281235968 | bytes 29622272 | tf_op jit(solution)/shard_map/dot_general | solution.py:127
  493.7 8.5 %copy.75 = bf16[512,5376]{0,1:T(8,128)(2,1)} copy(bf16[512,5376]{1,0:T(8,128)(2,1)} %convolution_convert_fusion) | data formatting | bytes 11010048
  502.2 17.0 %fusion.10 = (f32[512,8,2]{0,2,1:T(2,128)S(1)}, f32[8,128,2,512]{3,1,2,0:T(8,128)}) fusion(f32[512,2048]{0,1:T(8,128)} %copy.41, f32[512,8,2]{0,2,1:T(2,128)S(1)} %add_rsqrt_fusion, bf16[8,2,512,1536]{2,3,1,0:T(8,128)(2,1)} %fusion.1, bf16[1536,8,256]{2,0,1:T(8,128)(2,1)} %maximum_maximum_fusion), kind=kOutput, calls=%fused_computation.28 | convolution fusion | flops 3225411584 | bytes 36765696 | tf_op jit(solution)/shard_map/kgqj,jkd->qkgd/dot_general | solution.py:98
  519.3 6.7 %fusion.11 = f32[512,8,2,128]{0,3,2,1:T(8,128)} fusion(f32[8,128,2,512]{3,1,2,0:T(8,128)} %get-tuple-element.13, f32[512,2048]{0,1:T(8,128)} %copy.41, f32[512,8,2]{0,2,1:T(2,128)S(1)} %broadcast_multiply_fusion, f32[512,8,2]{0,2,1:T(2,128)S(1)} %add_rsqrt_fusion), kind=kLoop, calls=%fused_computation.29 | loop fusion | flops 5242880 | bytes 12648448 | tf_op jit(solution)/shard_map/mul | solution.py:27
  525.9 5.4 copy.57
  531.3 38.2 %reduce-scatter.4.cloned.1.call-done = bf16[2688,512]{1,0:T(8,128)(2,1)} async-done(((bf16[5376,512]{1,0:T(8,128)(2,1)}), bf16[2688,512]{1,0:T(8,128)(2,1)}) %reduce-scatter.4.cloned.1.call-update) | async-done | bytes 2752528
  569.5 4.6 copy.76
  574.1 4.6 convert_element_type.79
  (69 shorter events, 50.9 us)
Async XLA Ops:
  7.2 264.1 %copy-start = (bf16[2048,512]{1,0:T(8,128)(2,1)S(1)}, bf16[2048,512]{1,0:T(8,128)(2,1)}, u32[]{:S(2)}) copy-start(bf16[2048,512]{1,0:T(8,128)(2,1)} %param.11) | copy-start | bytes 6291460
  7.2 118.1 %all-gather.2.cloned.1.call-start = ((), (), s32[]{:S(2)}) async-start(), calls=%async_computation.1 | async-start | bytes 23396352 | tf_op jit(solution)/shard_map/all_gather | solution.py:39
  9.9 293.8 %all-reduce.2.cloned.1.call-start = ((), (), s32[]{:S(2)}) async-start(), calls=%async_computation.2 | async-start | bytes 1048576 | tf_op jit(solution)/shard_map/psum | solution.py:75
  143.7 6.2 %copy-start.8 = (f32[512,8]{0,1:T(8,128)}, f32[512,8]{0,1:T(8,128)S(1)}, u32[]{:S(2)}) copy-start(f32[512,8]{0,1:T(8,128)S(1)} %add_rsqrt_fusion.1) | copy-start | bytes 49156
  151.3 26.4 %collective-permute-start = (bf16[512,8,256]{2,0,1:T(8,128)(2,1)S(1)}, bf16[512,8,256]{2,0,1:T(8,128)(2,1)}, u32[]{:S(2)}, u32[]{:S(2)}) collective-permute-start(bf16[512,8,256]{2,0,1:T(8,128)(2,1)S(1)} %pad_maximum_fusion.1), channel_id=1, source_target_pairs={{0,2},{2,4},{4,6},{6,8},{8,10},{10,12},{12,14},{14,16},{16,18},{18... | collective-permute-start | bytes 6291464 | tf_op jit(solution)/shard_map/ppermute | solution.py:18
  177.8 28.7 %collective-permute-start.1 = (bf16[512,8,256]{2,0,1:T(8,128)(2,1)}, bf16[512,8,256]{2,0,1:T(8,128)(2,1)}, u32[]{:S(2)}, u32[]{:S(2)}) collective-permute-start(bf16[512,8,256]{2,0,1:T(8,128)(2,1)} %collective-permute-done), channel_id=1, source_target_pairs={{0,2},{2,4},{4,6},{6,8},{8,10},{10,12},{12,14},{14,16},{16,18},{18... | collective-permute-start | bytes 6291464 | tf_op jit(solution)/shard_map/ppermute | solution.py:18
  187.8 18.6 %copy-start.5 = (bf16[512,8,128]{2,0,1:T(8,128)(2,1)S(1)}, bf16[512,8,128]{2,0,1:T(8,128)(2,1)}, u32[]{:S(2)}) copy-start(bf16[512,8,128]{2,0,1:T(8,128)(2,1)} %copy.43) | copy-start | bytes 3145732
  192.0 19.8 %copy-start.6 = (pred[512,1536]{0,1:T(8,128)(4,1)}, pred[512,1536]{0,1:T(8,128)(4,1)S(1)}, u32[]{:S(2)}) copy-start(pred[512,1536]{0,1:T(8,128)(4,1)S(1)} %fusion.13) | copy-start | bytes 2359300
  192.0 19.8 %copy-start.2 = (f32[512,2048]{0,1:T(8,128)S(1)}, f32[512,2048]{0,1:T(8,128)}, u32[]{:S(2)}) copy-start(f32[512,2048]{0,1:T(8,128)} %copy.41) | copy-start | bytes 12582916
  271.2 2.4 copy-start.10
  271.2 33.9 %copy-start.11 = (s32[512]{0:T(512)S(1)}, s32[512]{0:T(512)}, u32[]{:S(2)}) copy-start(s32[512]{0:T(512)} %param.13) | copy-start | bytes 6148
  273.3 296.2 %reduce-scatter.4.cloned.1.call-start = ((), (), s32[]{:S(2)}) async-start(), calls=%async_computation.3 | async-start | bytes 8257536
  326.3 26.3 %copy-start.7 = (pred[512,1536]{0,1:T(8,128)(4,1)S(1)}, pred[512,1536]{0,1:T(8,128)(4,1)}, u32[]{:S(2)}) copy-start(pred[512,1536]{0,1:T(8,128)(4,1)} %copy-done.6) | copy-start | bytes 2359300
  407.7 31.1 %copy-start.3 = (f32[1536,8,128]{2,0,1:T(8,128)S(1)}, f32[1536,8,128]{2,0,1:T(8,128)}, u32[]{:S(2)}) copy-start(f32[1536,8,128]{2,0,1:T(8,128)} %fusion.3) | copy-start | bytes 18874372
  407.7 61.7 %slice-start = ((s8[6291456]{0:T(1024)(128)(4,1)}), s8[4194304]{0:T(1024)(128)(4,1)S(1)}, s32[]{:S(2)}) async-start(s8[6291456]{0:T(1024)(128)(4,1)} %bitcast.91), calls=%async_computation.4 | async-start | bytes 8388608
  410.3 59.1 %slice-start.1 = ((s8[6291456]{0:T(1024)(128)(4,1)}), s8[2097152]{0:T(1024)(128)(4,1)S(1)}, s32[]{:S(2)}) async-start(s8[6291456]{0:T(1024)(128)(4,1)} %bitcast.91), calls=%async_computation.5 | async-start | bytes 4194304
  410.3 28.5 %collective-permute-start.2 = (bf16[512,8,256]{2,0,1:T(8,128)(2,1)S(1)}, bf16[512,8,256]{2,0,1:T(8,128)(2,1)S(1)}, u32[]{:S(2)}, u32[]{:S(2)}) collective-permute-start(bf16[512,8,256]{2,0,1:T(8,128)(2,1)S(1)} %fusion.8), channel_id=1, source_target_pairs={{2,0},{4,2},{6,4},{8,6},{10,8},{12,10},{14,12},{16,14},{18,16},{20... | collective-permute-start | bytes 6291464 | tf_op jit(solution)/shard_map/ppermute | solution.py:18
  441.0 28.9 %copy-start.4 = (f32[512,8,128]{2,0,1:T(8,128)S(1)}, f32[512,8,128]{2,0,1:T(8,128)}, u32[]{:S(2)}) copy-start(f32[512,8,128]{2,0,1:T(8,128)} %copy.42) | copy-start | bytes 6291460
  441.0 28.9 %copy-start.9 = (f32[512,8]{0,1:T(8,128)S(1)}, f32[512,8]{0,1:T(8,128)}, u32[]{:S(2)}) copy-start(f32[512,8]{0,1:T(8,128)} %copy-done.8) | copy-start | bytes 49156
  441.0 28.4 %collective-permute-start.3 = (bf16[512,8,256]{2,0,1:T(8,128)(2,1)S(1)}, bf16[512,8,256]{2,0,1:T(8,128)(2,1)S(1)}, u32[]{:S(2)}, u32[]{:S(2)}) collective-permute-start(bf16[512,8,256]{2,0,1:T(8,128)(2,1)S(1)} %fusion.6), channel_id=1, source_target_pairs={{2,0},{4,2},{6,4},{8,6},{10,8},{12,10},{14,12},{16,14},{18,16},{20... | collective-permute-start | bytes 6291464 | tf_op jit(solution)/shard_map/ppermute | solution.py:18
  569.5 9.2 %copy-start.1 = (bf16[2048,512]{1,0:T(8,128)(2,1)S(1)}, bf16[2048,512]{1,0:T(8,128)(2,1)}, u32[]{:S(2)}) copy-start(bf16[2048,512]{1,0:T(8,128)(2,1)} %param.11) | copy-start | bytes 6291460
Sparse Core Ops, SparseCore 0:
  10.2 115.0 all-gather.1
  273.4 30.1 all-reduce.1
  502.4 67.0 reduce-scatter.3
where the time goes:
time: 592 us; the launch traced here: 586 us
  waiting for transfers between devices  273 us (46%)
  matrix products  146 us (25%)
  other arithmetic  103 us (17%)
  local copies, waits for them, and re-layouts  34.5 us (6%)
  starting transfers between devices  14.9 us (3%)
  between operations  14.4 us (2%)
    all_gather x1, waiting for transfers between devices, shards(): full_weight = lax.all_gather(stacked, 'seq', axis=0, tiled=True)  115 us
    ppermute x4, waiting for transfers between devices, passed_along(): lax.ppermute(value, axis, [(source, source + steps) for source in range(l...  89 us
    convert_element_type x1, other arithmetic, shards(): (attn_f * (d_weights - jnp.sum(attn_f * d_weights, axis=-1, keepdims=True...  40.6 us
    unnamed x4, waiting for transfers between devices  38.2 us
    psum x1, waiting for transfers between devices, shards(): lax.psum(partial_value.astype(jnp.bfloat16), 'head').astype(jnp.float32)  30.1 us
    dot_general x1, matrix products, shards(): jnp.einsum('qkgd,jkd->kgqj', attended_grad, value_block, preferred_elemen...  26.3 us
    convert_element_type x1, other arithmetic, shards(): (raised / jnp.sum(raised, axis=-1, keepdims=True)).astype(jnp.bfloat16)  26 us
    dot_general x1, matrix products, shards(): jnp.einsum('qkgd,jkd->kgqj', query_hat, key_block, preferred_element_type...  20.7 us
  transfers between devices with their start and end apart: 7, of which 7 were waited for; matrix products, arithmetic and copies ran while one was open for 6% of the time, Pallas kernels for 0%

commit v1 on v0

v1 whole, which is shorter than its diff:
```python
import functools

import jax
import jax.numpy as jnp
from jax import lax
from jax.experimental import pallas as pl
from jax.experimental.pallas import tpu as pltpu
from jax.sharding import PartitionSpec as P

HEAD_SIZE = 128
WINDOW_KEYS = 1024
TILE = 256
GROUPS = 4

norm_eps = 1e-06
softcap = 30.0
score_scale = 168.0 ** (-0.5)
log2_scale = score_scale * 1.4426950408889634

VMEM_LIMIT = 48 * 1024 * 1024
NT = (((1,), (1,)), ((), ()))
TN = (((0,), (0,)), ((), ()))


def passed_along(value, axis, steps):
    count = lax.axis_size(axis)
    leading, last = (max(0, -steps), min(count, count - steps))
    return lax.ppermute(value, axis, [(source, source + steps) for source in range(leading, last)])


def swapped(value, axis):
    return lax.ppermute(value, axis, [(0, 1), (1, 0)])


def dot(a, b, dims=(((1,), (0,)), ((), ()))):
    return lax.dot_general(a, b, dims, preferred_element_type=jnp.float32)


def normalized_rows(value_rows):
    inverse = lax.rsqrt(jnp.mean(value_rows * value_rows, axis=-1, keepdims=True) + norm_eps)
    return (value_rows * inverse, inverse)


def unit_norm_backward(unit, inverse, upstream):
    return inverse * (upstream - unit * jnp.mean(unit * upstream, axis=-1, keepdims=True))


def prep_kernel(raw_ref, kv_ref):
    unit, _ = normalized_rows(raw_ref[:, :HEAD_SIZE])
    kv_ref[:, :HEAD_SIZE] = unit.astype(jnp.bfloat16)
    kv_ref[:, HEAD_SIZE:] = raw_ref[:, HEAD_SIZE:].astype(jnp.bfloat16)


def post_kernel(raw_ref, arrived_ref, own_ref, out_ref):
    unit, inverse = normalized_rows(raw_ref[:, :HEAD_SIZE])
    total = arrived_ref[...].astype(jnp.float32) + own_ref[...]
    out_ref[:, :HEAD_SIZE] = unit_norm_backward(unit, inverse, total[:, :HEAD_SIZE]).astype(
        jnp.bfloat16
    )
    out_ref[:, HEAD_SIZE:] = total[:, HEAD_SIZE:].astype(jnp.bfloat16)


def stacked_rows(ref, rows, group):
    parts = [ref[rows, g * HEAD_SIZE : (g + 1) * HEAD_SIZE] for g in range(group)]
    return jnp.concatenate(parts, axis=0)


def forward_kernel(reach, group, valid_ref, q_ref, *refs):
    kv_refs, (o_ref, sum_ref) = refs[: reach + 1], refs[reach + 1 :]
    tokens = q_ref.shape[0]
    spans = WINDOW_KEYS // TILE + 1
    rows = group * TILE
    for block in range(tokens // TILE):
        here = slice(block * TILE, (block + 1) * TILE)
        unit, _ = normalized_rows(stacked_rows(q_ref, here, group).astype(jnp.float32))
        q_hat = unit.astype(jnp.bfloat16)
        total = jnp.zeros((rows, 2 * HEAD_SIZE), jnp.float32)
        for c in range(spans):
            slot, low = divmod((block + c) * TILE, tokens)
            kv_ref = kv_refs[slot]
            key = kv_ref[low : low + TILE, :HEAD_SIZE]
            value = kv_ref[low : low + TILE, HEAD_SIZE:]
            raised = jnp.exp2(dot(q_hat, key, NT) * log2_scale)
            if c in (0, spans - 1):
                i = lax.broadcasted_iota(jnp.int32, (rows, TILE), 0) % TILE
                t = lax.broadcasted_iota(jnp.int32, (rows, TILE), 1)
                raised = jnp.where((t > i) if c == 0 else (t <= i), raised, 0.0)
            flag = jnp.full((TILE, HEAD_SIZE), valid_ref[slot], jnp.float32).astype(jnp.bfloat16)
            total += dot(raised.astype(jnp.bfloat16), jnp.concatenate([value, flag], axis=1))
        sums = total[:, HEAD_SIZE:]
        out = (total[:, :HEAD_SIZE] / sums).astype(jnp.bfloat16)
        for g in range(group):
            o_ref[here, g * HEAD_SIZE : (g + 1) * HEAD_SIZE] = out[g * TILE : (g + 1) * TILE]
        sum_ref[:, block * rows : (block + 1) * rows] = sums.T[:8]


def backward_kernel(reach, group, valid_ref, q_ref, o_ref, g_ref, sum_ref, *refs):
    kv_refs = refs[: reach + 1]
    qg_ref = refs[reach + 1]
    d_refs = refs[reach + 2 : 2 * reach + 3]
    acc_ref = refs[2 * reach + 3]
    tokens = q_ref.shape[0]
    spans = WINDOW_KEYS // TILE + 1
    rows = group * TILE
    acc_ref[...] = jnp.zeros_like(acc_ref)
    for block in range(tokens // TILE):
        here = slice(block * TILE, (block + 1) * TILE)
        unit, inverse = normalized_rows(stacked_rows(q_ref, here, group).astype(jnp.float32))
        q_hat = unit.astype(jnp.bfloat16)
        grad = stacked_rows(g_ref, here, group)
        out = stacked_rows(o_ref, here, group)
        product = grad.astype(jnp.float32) * out.astype(jnp.float32)
        delta = jnp.sum(product.T, axis=0, keepdims=True)
        inv = 1.0 / sum_ref[0:1, block * rows : (block + 1) * rows]
        dq = jnp.zeros((HEAD_SIZE, rows), jnp.float32)
        for c in range(spans):
            at = (block + c) * TILE
            slot, low = divmod(at, tokens)
            kv_ref = kv_refs[slot]
            key = kv_ref[low : low + TILE, :HEAD_SIZE]
            value = kv_ref[low : low + TILE, HEAD_SIZE:]
            raised = jnp.exp2(dot(key, q_hat, NT) * log2_scale)
            if c in (0, spans - 1):
                t = lax.broadcasted_iota(jnp.int32, (TILE, rows), 0)
                i = lax.broadcasted_iota(jnp.int32, (TILE, rows), 1) % TILE
                raised = jnp.where((t > i) if c == 0 else (t <= i), raised, 0.0)
            attn = raised * (inv * valid_ref[slot])
            attn16 = attn.astype(jnp.bfloat16)
            d_scores = (attn * (dot(value, grad, NT) - delta)).astype(jnp.bfloat16)
            acc_ref[at : at + TILE, :HEAD_SIZE] += dot(d_scores, q_hat)
            acc_ref[at : at + TILE, HEAD_SIZE:] += dot(attn16, grad)
            dq += dot(key, d_scores, TN)
        result = unit_norm_backward(unit, inverse, dq.T * score_scale)
        for g in range(group):
            qg_ref[here, g * HEAD_SIZE : (g + 1) * HEAD_SIZE] = result[g * TILE : (g + 1) * TILE]
    for slot in range(reach + 1):
        part = acc_ref[slot * tokens : (slot + 1) * tokens]
        d_refs[slot][:, :HEAD_SIZE] = (part[:, :HEAD_SIZE] * score_scale).astype(d_refs[slot].dtype)
        d_refs[slot][:, HEAD_SIZE:] = part[:, HEAD_SIZE:].astype(d_refs[slot].dtype)


def params():
    return pltpu.CompilerParams(vmem_limit_bytes=VMEM_LIMIT)


def columns(tokens, width, first=0):
    return pl.BlockSpec((tokens, width), lambda h: (0, first + h))


def prep(raw):
    tokens, width = raw.shape
    spec = columns(tokens, 2 * HEAD_SIZE)
    return pl.pallas_call(
        prep_kernel,
        grid=(width // (2 * HEAD_SIZE),),
        in_specs=[spec],
        out_specs=spec,
        out_shape=jax.ShapeDtypeStruct((tokens, width), jnp.bfloat16),
        compiler_params=params(),
        cost_estimate=pl.CostEstimate(
            flops=6 * tokens * width, bytes_accessed=6 * tokens * width, transcendentals=0
        ),
    )(raw)


def post(raw, arrived, own):
    tokens, width = raw.shape
    spec = columns(tokens, 2 * HEAD_SIZE)
    return pl.pallas_call(
        post_kernel,
        grid=(width // (2 * HEAD_SIZE),),
        in_specs=[spec] * 3,
        out_specs=spec,
        out_shape=jax.ShapeDtypeStruct((tokens, width), jnp.bfloat16),
        compiler_params=params(),
        cost_estimate=pl.CostEstimate(
            flops=12 * tokens * width, bytes_accessed=12 * tokens * width, transcendentals=0
        ),
    )(raw, arrived, own)


def attention_forward(valid, queries, window, first, heads, group):
    tokens = queries.shape[0]
    reach = len(window) - 1
    wide = group * HEAD_SIZE
    work = heads * group * tokens * (WINDOW_KEYS + TILE)
    return pl.pallas_call(
        functools.partial(forward_kernel, reach, group),
        grid=(heads,),
        in_specs=[pl.BlockSpec(memory_space=pltpu.SMEM), columns(tokens, wide, first)]
        + [columns(tokens, 2 * HEAD_SIZE)] * (reach + 1),
        out_specs=[
            columns(tokens, wide),
            pl.BlockSpec((8, group * tokens), lambda h: (h, 0)),
        ],
        out_shape=[
            jax.ShapeDtypeStruct((tokens, heads * wide), jnp.bfloat16),
            jax.ShapeDtypeStruct((heads * 8, group * tokens), jnp.float32),
        ],
        compiler_params=params(),
        cost_estimate=pl.CostEstimate(
            flops=8 * HEAD_SIZE * work, bytes_accessed=10 * tokens * heads * wide, transcendentals=work
        ),
    )(valid, queries, *window)


def attention_backward(valid, queries, attended, grad, sums, window, first, heads, group):
    tokens = queries.shape[0]
    reach = len(window) - 1
    wide = group * HEAD_SIZE
    work = heads * group * tokens * (WINDOW_KEYS + TILE)
    kinds = [jnp.bfloat16] + [jnp.float32] * reach
    return pl.pallas_call(
        functools.partial(backward_kernel, reach, group),
        grid=(heads,),
        in_specs=[
            pl.BlockSpec(memory_space=pltpu.SMEM),
            columns(tokens, wide, first),
            columns(tokens, wide),
            columns(tokens, wide, first),
            pl.BlockSpec((8, group * tokens), lambda h: (h, 0)),
        ]
        + [columns(tokens, 2 * HEAD_SIZE)] * (reach + 1),
        out_specs=[columns(tokens, wide)] + [columns(tokens, 2 * HEAD_SIZE)] * (reach + 1),
        out_shape=[jax.ShapeDtypeStruct((tokens, heads * wide), jnp.float32)]
        + [jax.ShapeDtypeStruct((tokens, heads * 2 * HEAD_SIZE), kind) for kind in kinds],
        scratch_shapes=[pltpu.VMEM(((reach + 1) * tokens, 2 * HEAD_SIZE), jnp.float32)],
        compiler_params=params(),
        cost_estimate=pl.CostEstimate(
            flops=16 * HEAD_SIZE * work, bytes_accessed=24 * tokens * heads * wide, transcendentals=work
        ),
    )(valid, queries, attended, grad, sums, *window)


def shards(inputs, queries, key_matrix, value_matrix, readout, token_mask, targets):
    tokens = inputs.shape[0]
    kv_width = key_matrix.shape[1]
    kv_heads = kv_width // HEAD_SIZE
    q_heads = queries.shape[1] // HEAD_SIZE
    group = q_heads // kv_heads
    reach = WINDOW_KEYS // tokens
    groups = min(GROUPS, kv_heads)
    heads = kv_heads // groups
    wide = heads * group * HEAD_SIZE
    position = lax.axis_index("seq")
    valid = (position >= reach - jnp.arange(reach + 1)).astype(jnp.float32)

    weights, raws, windows, outs, sums = [], [], [], [], []
    partial = None
    for n in range(groups):
        parts = []
        for h in range(n * heads, (n + 1) * heads):
            cols = slice(h * HEAD_SIZE, (h + 1) * HEAD_SIZE)
            parts += [key_matrix[:, cols], value_matrix[:, cols]]
        weight = lax.all_gather(jnp.concatenate(parts, axis=1), "seq", axis=0, tiled=True)
        raw = dot(inputs, weight)
        moving = prep(raw)
        window = [moving]
        for _ in range(reach):
            moving = passed_along(moving, "seq", 1)
            window.insert(0, moving)
        out, total = attention_forward(valid, queries, window, n * heads, heads, group)
        term = dot(out, readout[n * wide : (n + 1) * wide])
        partial = term if partial is None else partial + term
        weights.append(weight)
        raws.append(raw)
        windows.append(window)
        outs.append(out)
        sums.append(total)

    mine = partial.astype(jnp.bfloat16)
    if lax.axis_size("head") == 2:
        logits = mine.astype(jnp.float32) + swapped(mine, "head").astype(jnp.float32)
    else:
        logits = lax.psum(mine, "head").astype(jnp.float32)
    capped = softcap * jnp.tanh(logits / softcap)
    expo = jnp.exp(capped)
    probs = expo / jnp.sum(expo, axis=-1, keepdims=True)
    onehot = (targets[:, None] == jnp.arange(logits.shape[1], dtype=jnp.int32)[None, :]).astype(
        jnp.float32
    )
    chosen = token_mask.astype(jnp.float32)[:, None]
    dlogits = (chosen * (probs - onehot) * (1.0 - (capped / softcap) ** 2)).astype(jnp.bfloat16)
    attended_grad = dot(dlogits, readout, NT).astype(jnp.bfloat16)

    query_grads, grads = [], []
    for n in range(groups):
        query_grad, *pieces = attention_backward(
            valid, queries, outs[n], attended_grad, sums[n], windows[n], n * heads, heads, group
        )
        query_grads.append(query_grad)
        total = pieces[0]
        for slot in range(1, reach):
            arrived = passed_along(total, "seq", -1).astype(jnp.float32)
            total = (arrived + pieces[slot]).astype(jnp.bfloat16)
        grads.append(post(raws[n], passed_along(total, "seq", -1), pieces[reach]))

    def product(low, size):
        result = None
        for grad, weight in zip(grads, weights):
            term = dot(grad, lax.dynamic_slice_in_dim(weight, low, size, 0), NT)
            result = term if result is None else result + term
        return result.astype(jnp.bfloat16)

    model = weights[0].shape[0]
    if lax.axis_size("head") == 2:
        half = model // 2
        me = lax.axis_index("head")
        arrived = swapped(product((1 - me) * half, half), "head")
        input_grad = product(me * half, half).astype(jnp.float32) + arrived.astype(jnp.float32)
    else:
        input_grad = lax.psum_scatter(
            product(0, model), "head", scatter_dimension=1, tiled=True
        ).astype(jnp.float32)
    return (jnp.concatenate(query_grads, axis=1), input_grad)


def solution(mesh):
    in_specs = (
        P("seq", None),
        P("seq", "head"),
        P("seq", "head"),
        P("seq", "head"),
        P("head", None),
        P("seq"),
        P("seq"),
    )
    out_specs = (P("seq", "head"), P("seq", "head"))
    return jax.shard_map(shards, mesh=mesh, in_specs=in_specs, out_specs=out_specs, check_vma=False)
```

time: 592 us -> 521 us (0.88)
  other arithmetic: 103 us -> 23.4 us
  Pallas kernels: 0 us -> 69.4 us
  matrix products: 146 us -> 81.4 us
  starting transfers between devices: 14.9 us -> 50.6 us
  local copies, waits for them, and re-layouts: 34.5 us -> 11 us
  waiting for transfers between devices: 273 us -> 264 us
    all_gather x1 -> x4, waiting for transfers between devices: 115 us -> 207 us  [shards(): lax.all_gather(jnp.concatenate(parts, axis=1), 'seq', axis=0, tiled=True)]
    ppermute x4 -> x16, waiting for transfers between devices: 89 us -> 9.41 us  [passed_along(): lax.ppermute(value, axis, [(source, source + steps) for source in range(l...]
    convert_element_type x6 -> x5, other arithmetic: 76.6 us -> 2.73 us  [the longest x4 2.73 us: shards(): total = (arrived + pieces[slot]).astype(jnp.bfloat16)]
    pallas_call x0 -> x16, Pallas kernels: none -> 69.4 us  [the longest x4 43.2 us: attention_backward(): pl.pallas_call(functools.partial(backward_kernel, reach, group), grid=(he...]
    dot_general x10 -> x17, matrix products: 146 us -> 81.4 us  [dot(): return lax.dot_general(a, b, dims, preferred_element_type=jnp.float32)]
    ppermute x0 -> x2, waiting for transfers between devices: none -> 47.6 us  [swapped(): return lax.ppermute(value, axis, [(0, 1), (1, 0)])]
    unnamed x4, waiting for transfers between devices: 38.2 us -> 0.07 us
    ppermute x4 -> x16, starting transfers between devices: 14.6 us -> 48.1 us  [passed_along(): lax.ppermute(value, axis, [(source, source + steps) for source in range(l...]
  transfers between devices with their start and end apart: 7 -> 22, of which waited for: 7 -> 8; matrix products, arithmetic and copies ran while one was open for 6% -> 15% of each run, Pallas kernels for 0% -> 10%
where the time goes in v1:
time: 521 us; the launch traced here: 515 us
  waiting for transfers between devices  264 us (51%)
  matrix products  81.4 us (16%)
  Pallas kernels  69.4 us (13%)
  starting transfers between devices  50.6 us (10%)
  other arithmetic  23.4 us (4%)
  between operations  14.9 us (3%)
  local copies, waits for them, and re-layouts  11 us (2%)
    all_gather x4, waiting for transfers between devices, shards(): lax.all_gather(jnp.concatenate(parts, axis=1), 'seq', axis=0, tiled=True)  207 us
    dot_general x17, matrix products, dot(): return lax.dot_general(a, b, dims, preferred_element_type=jnp.float32)  81.4 us
    ppermute x16, starting transfers between devices, passed_along(): lax.ppermute(value, axis, [(source, source + steps) for source in range(l...  48.1 us
    ppermute x2, waiting for transfers between devices, swapped(): return lax.ppermute(value, axis, [(0, 1), (1, 0)])  47.6 us
    pallas_call x4, Pallas kernels, attention_backward(): pl.pallas_call(functools.partial(backward_kernel, reach, group), grid=(he...  43.2 us
    pallas_call x4, Pallas kernels, attention_forward(): pl.pallas_call(functools.partial(forward_kernel, reach, group), grid=(hea...  19.9 us
    add x1, other arithmetic, shards(): product(me * half, half).astype(jnp.float32) + arrived.astype(jnp.float32)  11.7 us
  transfers between devices with their start and end apart: 22, of which 8 were waited for; matrix products, arithmetic and copies ran while one was open for 15% of the time, Pallas kernels for 10%

profile of v1, /device:TPU:13, one launch (start us, length us, event | category | flops | bytes accessed | tf_op | source)
XLA Modules:
  0.0 514.8 jit_solution(8379967896459757373)
XLA Ops:
  12.1 56.8 %all-gather.11.cloned.1.call-done = bf16[5376,512]{1,0:T(8,128)(2,1)} async-done(((bf16[336,512]{1,0:T(8,128)(2,1)}), bf16[5376,512]{1,0:T(8,128)(2,1)}) %all-gather.11.cloned.1.call-update) | async-done | bytes 5505040 | tf_op jit(solution)/shard_map/all_gather | solution.py:255
  68.9 6.7 %convolution_bitcast_fusion.raw_ref = f32[512,512]{1,0:T(8,128)S(1)} fusion(bf16[512,5376]{1,0:T(8,128)(2,1)} %param.7, bf16[5376,512]{1,0:T(8,128)(2,1)} %all-gather.11.cloned.1.call-done), kind=kOutput, calls=%fused_computation.21 | convolution fusion | flops 2818572288 | bytes 12058624 | tf_op jit(solution)/shard_map/dot_general | solution.py:36
  79.7 50.7 %all-gather.7.cloned.1.call-done = bf16[5376,512]{1,0:T(8,128)(2,1)} async-done(((bf16[336,512]{1,0:T(8,128)(2,1)}), bf16[5376,512]{1,0:T(8,128)(2,1)}) %all-gather.7.cloned.1.call-update) | async-done | bytes 5505040 | tf_op jit(solution)/shard_map/all_gather | solution.py:255
  130.4 6.7 %convolution_bitcast_fusion.2.raw_ref = f32[512,512]{1,0:T(8,128)S(1)} fusion(bf16[512,5376]{1,0:T(8,128)(2,1)} %param.7, bf16[5376,512]{1,0:T(8,128)(2,1)} %all-gather.7.cloned.1.call-done), kind=kOutput, calls=%fused_computation.23 | convolution fusion | flops 2818572288 | bytes 12058624 | tf_op jit(solution)/shard_map/dot_general | solution.py:36
  141.2 51.6 %all-gather.9.cloned.1.call-done = bf16[5376,512]{1,0:T(8,128)(2,1)} async-done(((bf16[336,512]{1,0:T(8,128)(2,1)}), bf16[5376,512]{1,0:T(8,128)(2,1)}) %all-gather.9.cloned.1.call-update) | async-done | bytes 5505040 | tf_op jit(solution)/shard_map/all_gather | solution.py:255
  192.9 6.7 %convolution_bitcast_fusion.1.raw_ref = f32[512,512]{1,0:T(8,128)S(1)} fusion(bf16[512,5376]{1,0:T(8,128)(2,1)} %param.7, bf16[5376,512]{1,0:T(8,128)(2,1)} %all-gather.9.cloned.1.call-done), kind=kOutput, calls=%fused_computation.22 | convolution fusion | flops 2818572288 | bytes 12058624 | tf_op jit(solution)/shard_map/dot_general | solution.py:36
  205.3 47.9 %all-gather.5.cloned.1.call-done = bf16[5376,512]{1,0:T(8,128)(2,1)} async-done(((bf16[336,512]{1,0:T(8,128)(2,1)}), bf16[5376,512]{1,0:T(8,128)(2,1)}) %all-gather.5.cloned.1.call-update) | async-done | bytes 5505040 | tf_op jit(solution)/shard_map/all_gather | solution.py:255
  253.2 6.7 %convolution_bitcast_fusion.3.raw_ref = f32[512,512]{1,0:T(8,128)S(1)} fusion(bf16[512,5376]{1,0:T(8,128)(2,1)} %param.7, bf16[5376,512]{1,0:T(8,128)(2,1)} %all-gather.5.cloned.1.call-done), kind=kOutput, calls=%fused_computation.24 | convolution fusion | flops 2818572288 | bytes 12058624 | tf_op jit(solution)/shard_map/dot_general | solution.py:36
  272.4 5.4 %collective-permute-start.1 = (bf16[512,512]{1,0:T(8,128)(2,1)}, bf16[512,512]{1,0:T(8,128)(2,1)S(1)}, u32[]{:S(2)}, u32[]{:S(2)}) collective-permute-start(bf16[512,512]{1,0:T(8,128)(2,1)} %collective-permute-done.refs_1_), channel_id=1, source_target_pairs={{0,2},{2,4},{4,6},{6,8},{8,10},{10,12},{12,14},{14,16},{16,18},{18... | collective-permute-start | bytes 1572872 | tf_op jit(solution)/shard_map/ppermute | solution.py:28
  308.4 11.7 %collective-permute-done.8 = bf16[512,512]{0,1:T(8,128)(2,1)} collective-permute-done((bf16[512,512]{0,1:T(8,128)(2,1)}, bf16[512,512]{0,1:T(8,128)(2,1)}, u32[]{:S(2)}, u32[]{:S(2)}) %collective-permute-start.8) | collective-permute-done | bytes 524320 | tf_op jit(solution)/shard_map/ppermute | solution.py:32
  321.6 5.1 convolution_convert_fusion.g_ref
  326.7 11.2 %shard_map.97 = (f32[512,512]{1,0:T(8,128)S(1)}, bf16[512,512]{1,0:T(8,128)(2,1)}, f32[512,512]{1,0:T(8,128)S(1)}, f32[512,512]{1,0:T(8,128)S(1)}) custom-call(f32[3]{0:T(128)S(1)} %compare_convert_fusion.valid_ref, bf16[512,2048]{1,0:T(8,128)(2,1)} %q_ref.15, bf16[512,512]{1,0:T(8,128)(2,1)S(1)} %copy-done.16, ...), custom_call_target="tpu_custom_call" | custom-call | flops 5368709120 | bytes 6291456 | tf_op jit(solution)/shard_map/pallas_call | solution.py:213
  342.6 10.7 %shard_map.96 = (f32[512,512]{1,0:T(8,128)S(1)}, bf16[512,512]{1,0:T(8,128)(2,1)S(1)}, f32[512,512]{1,0:T(8,128)S(1)}, f32[512,512]{1,0:T(8,128)S(1)}) custom-call(f32[3]{0:T(128)S(1)} %compare_convert_fusion.valid_ref, bf16[512,2048]{1,0:T(8,128)(2,1)} %q_ref.15, bf16[512,512]{1,0:T(8,128)(2,1)S(1)} %copy-done.14, ...), custom_call_target="tpu_custom_call" | custom-call | flops 5368709120 | bytes 6291456 | tf_op jit(solution)/shard_map/pallas_call | solution.py:213
  356.3 10.8 %shard_map.94 = (f32[512,512]{1,0:T(8,128)S(1)}, bf16[512,512]{1,0:T(8,128)(2,1)S(1)}, f32[512,512]{1,0:T(8,128)S(1)}, f32[512,512]{1,0:T(8,128)S(1)}) custom-call(f32[3]{0:T(128)S(1)} %compare_convert_fusion.valid_ref, bf16[512,2048]{1,0:T(8,128)(2,1)} %q_ref.15, bf16[512,512]{1,0:T(8,128)(2,1)S(1)} %copy-done.10, ...), custom_call_target="tpu_custom_call" | custom-call | flops 5368709120 | bytes 6291456 | tf_op jit(solution)/shard_map/pallas_call | solution.py:213
  370.3 10.5 %shard_map.95 = (f32[512,512]{1,0:T(8,128)S(1)}, bf16[512,512]{1,0:T(8,128)(2,1)S(1)}, f32[512,512]{1,0:T(8,128)S(1)}, f32[512,512]{1,0:T(8,128)S(1)}) custom-call(f32[3]{0:T(128)S(1)} %compare_convert_fusion.valid_ref, bf16[512,2048]{1,0:T(8,128)(2,1)} %q_ref.15, bf16[512,512]{1,0:T(8,128)(2,1)S(1)} %copy-done.12, ...), custom_call_target="tpu_custom_call" | custom-call | flops 5368709120 | bytes 6291456 | tf_op jit(solution)/shard_map/pallas_call | solution.py:213
  399.1 5.5 %collective-permute-done.10.arrived_ref = bf16[512,512]{1,0:T(8,128)(2,1)S(1)} collective-permute-done((bf16[512,512]{1,0:T(8,128)(2,1)S(1)}, bf16[512,512]{1,0:T(8,128)(2,1)S(1)}, u32[]{:S(2)}, u32[]{:S(2)}) %collective-permute-start.10) | collective-permute-done | bytes 524320 | tf_op jit(solution)/shard_map/ppermute | solution.py:28
  405.5 5.8 %fusion.8 = f32[512,2688]{1,0:T(8,128)} fusion(bf16[512,512]{1,0:T(8,128)(2,1)S(1)} %shard_map.98, bf16[5376,512]{1,0:T(8,128)(2,1)} %all-gather.5.cloned.1.call-done, s32[]{:T(128)S(6)} %select_n.5), kind=kOutput, calls=%fused_computation.11 | convolution fusion | flops 1409286144 | bytes 8781828 | tf_op jit(solution)/shard_map/dot_general | solution.py:36
  412.1 5.9 %fusion.6 = f32[512,2688]{1,0:T(8,128)} fusion(bf16[512,512]{1,0:T(8,128)(2,1)S(1)} %shard_map.99, bf16[5376,512]{1,0:T(8,128)(2,1)} %all-gather.7.cloned.1.call-done, s32[]{:T(128)S(6)} %select_n.5), kind=kOutput, calls=%fused_computation.9 | convolution fusion | flops 1409286144 | bytes 8781828 | tf_op jit(solution)/shard_map/dot_general | solution.py:36
  418.7 6.3 %fusion.4 = f32[512,2688]{1,0:T(8,128)} fusion(bf16[512,512]{1,0:T(8,128)(2,1)S(1)} %shard_map.100, bf16[5376,512]{1,0:T(8,128)(2,1)} %all-gather.9.cloned.1.call-done, s32[]{:T(128)S(6)} %select_n.5), kind=kOutput, calls=%fused_computation.7 | convolution fusion | flops 1409286144 | bytes 8781828 | tf_op jit(solution)/shard_map/dot_general | solution.py:36
  425.8 8.4 %add_convert_fusion = bf16[512,2688]{1,0:T(8,128)(2,1)} fusion(f32[512,2688]{1,0:T(8,128)} %fusion.4, f32[512,2688]{1,0:T(8,128)S(1)} %bitcast.30, f32[512,2688]{1,0:T(8,128)} %fusion.6, bf16[512,512]{1,0:T(8,128)(2,1)S(1)} %shard_map.101, bf16[5376,512]{1,0:T(8,128)(2,1)} %all-gather.11.cloned.1.call-done, s32[]{:T(128)S(6)} %select_n.5), kind=kOutput, calls=%fused_computation.1 | convolution fusion | flops 1414791168 | bytes 22544388 | tf_op jit(solution)/shard_map/dot_general | solution.py:36
  439.7 6.1 %fusion.16 = f32[512,2688]{1,0:T(8,128)} fusion(bf16[512,512]{1,0:T(8,128)(2,1)S(1)} %shard_map.98, bf16[5376,512]{1,0:T(8,128)(2,1)} %all-gather.5.cloned.1.call-done, s32[]{:T(128)S(6)} %select_n.4), kind=kOutput, calls=%fused_computation.19 | convolution fusion | flops 1409286144 | bytes 8781828 | tf_op jit(solution)/shard_map/dot_general | solution.py:36
  445.8 6.0 %fusion.14 = f32[512,2688]{1,0:T(8,128)} fusion(bf16[512,512]{1,0:T(8,128)(2,1)S(1)} %shard_map.99, bf16[5376,512]{1,0:T(8,128)(2,1)} %all-gather.7.cloned.1.call-done, s32[]{:T(128)S(6)} %select_n.4), kind=kOutput, calls=%fused_computation.17 | convolution fusion | flops 1409286144 | bytes 8781828 | tf_op jit(solution)/shard_map/dot_general | solution.py:36
  460.1 35.9 %collective-permute-done.17 = bf16[512,2688]{1,0:T(8,128)(2,1)} collective-permute-done((bf16[512,2688]{1,0:T(8,128)(2,1)}, bf16[512,2688]{1,0:T(8,128)(2,1)}, u32[]{:S(2)}, u32[]{:S(2)}) %collective-permute-start.17) | collective-permute-done | bytes 2752544 | tf_op jit(solution)/shard_map/ppermute | solution.py:32
  496.1 11.7 %convert_add_fusion = f32[512,2688]{1,0:T(8,128)} fusion(bf16[512,2688]{1,0:T(8,128)(2,1)} %collective-permute-done.17, f32[512,2688]{1,0:T(8,128)} %fusion.10, f32[512,2688]{1,0:T(8,128)} %fusion.12, f32[512,2688]{1,0:T(8,128)} %fusion.16, f32[512,2688]{1,0:T(8,128)} %fusion.14), kind=kLoop, calls=%fused_computation | loop fusion | flops 9633792 | bytes 30277632 | tf_op jit(solution)/shard_map/add | solution.py:310
  (142 shorter events, 109.0 us)
Async XLA Ops:
  7.2 61.8 %all-gather.11.cloned.1.call-start = ((), (), s32[]{:S(2)}) async-start(), calls=%async_computation.3 | async-start | bytes 5849088 | tf_op jit(solution)/shard_map/all_gather | solution.py:255
  9.6 120.9 %all-gather.7.cloned.1.call-start = ((), (), s32[]{:S(2)}) async-start(), calls=%async_computation.1 | async-start | bytes 5849088 | tf_op jit(solution)/shard_map/all_gather | solution.py:255
  10.4 182.4 %all-gather.9.cloned.1.call-start = ((), (), s32[]{:S(2)}) async-start(), calls=%async_computation.2 | async-start | bytes 5849088 | tf_op jit(solution)/shard_map/all_gather | solution.py:255
  11.3 241.9 %all-gather.5.cloned.1.call-start = ((), (), s32[]{:S(2)}) async-start(), calls=%async_computation | async-start | bytes 5849088 | tf_op jit(solution)/shard_map/all_gather | solution.py:255
  76.1 191.8 %collective-permute-start.6 = (bf16[512,512]{1,0:T(8,128)(2,1)S(1)}, bf16[512,512]{1,0:T(8,128)(2,1)}, u32[]{:S(2)}, u32[]{:S(2)}) collective-permute-start(bf16[512,512]{1,0:T(8,128)(2,1)S(1)} %shard_map.92.refs_2_), channel_id=1, source_target_pairs={{0,2},{2,4},{4,6},{6,8},{8,10},{10,12},{12,14},{14,16},{16,18},{18... | collective-permute-start | bytes 1572872 | tf_op jit(solution)/shard_map/ppermute | solution.py:28
  137.6 132.6 %collective-permute-start.2 = (bf16[512,512]{1,0:T(8,128)(2,1)S(1)}, bf16[512,512]{1,0:T(8,128)(2,1)}, u32[]{:S(2)}, u32[]{:S(2)}) collective-permute-start(bf16[512,512]{1,0:T(8,128)(2,1)S(1)} %shard_map.88.refs_2_), channel_id=1, source_target_pairs={{0,2},{2,4},{4,6},{6,8},{8,10},{10,12},{12,14},{14,16},{16,18},{18... | collective-permute-start | bytes 1572872 | tf_op jit(solution)/shard_map/ppermute | solution.py:28
  201.6 64.0 %collective-permute-start.4 = (bf16[512,512]{1,0:T(8,128)(2,1)}, bf16[512,512]{1,0:T(8,128)(2,1)}, u32[]{:S(2)}, u32[]{:S(2)}) collective-permute-start(bf16[512,512]{1,0:T(8,128)(2,1)} %shard_map.90.refs_2_), channel_id=1, source_target_pairs={{0,2},{2,4},{4,6},{6,8},{8,10},{10,12},{12,14},{14,16},{16,18},{18... | collective-permute-start | bytes 1572872 | tf_op jit(solution)/shard_map/ppermute | solution.py:28
  262.0 10.4 %collective-permute-start = (bf16[512,512]{1,0:T(8,128)(2,1)}, bf16[512,512]{1,0:T(8,128)(2,1)}, u32[]{:S(2)}, u32[]{:S(2)}) collective-permute-start(bf16[512,512]{1,0:T(8,128)(2,1)} %shard_map.86.refs_2_), channel_id=1, source_target_pairs={{0,2},{2,4},{4,6},{6,8},{8,10},{10,12},{12,14},{14,16},{16,18},{18... | collective-permute-start | bytes 1572872 | tf_op jit(solution)/shard_map/ppermute | solution.py:28
  265.6 12.2 %collective-permute-start.5 = (bf16[512,512]{1,0:T(8,128)(2,1)}, bf16[512,512]{1,0:T(8,128)(2,1)}, u32[]{:S(2)}, u32[]{:S(2)}) collective-permute-start(bf16[512,512]{1,0:T(8,128)(2,1)} %collective-permute-done.4.refs_1_), channel_id=1, source_target_pairs={{0,2},{2,4},{4,6},{6,8},{8,10},{10,12},{12,14},{14,16},{16,18},{18... | collective-permute-start | bytes 1572872 | tf_op jit(solution)/shard_map/ppermute | solution.py:28
  267.8 26.5 %collective-permute-start.7 = (bf16[512,512]{1,0:T(8,128)(2,1)}, bf16[512,512]{1,0:T(8,128)(2,1)S(1)}, u32[]{:S(2)}, u32[]{:S(2)}) collective-permute-start(bf16[512,512]{1,0:T(8,128)(2,1)} %collective-permute-done.6.refs_1_), channel_id=1, source_target_pairs={{0,2},{2,4},{4,6},{6,8},{8,10},{10,12},{12,14},{14,16},{16,18},{18... | collective-permute-start | bytes 1572872 | tf_op jit(solution)/shard_map/ppermute | solution.py:28
  270.2 18.7 %collective-permute-start.3 = (bf16[512,512]{1,0:T(8,128)(2,1)}, bf16[512,512]{1,0:T(8,128)(2,1)S(1)}, u32[]{:S(2)}, u32[]{:S(2)}) collective-permute-start(bf16[512,512]{1,0:T(8,128)(2,1)} %collective-permute-done.2.refs_1_), channel_id=1, source_target_pairs={{0,2},{2,4},{4,6},{6,8},{8,10},{10,12},{12,14},{14,16},{16,18},{18... | collective-permute-start | bytes 1572872 | tf_op jit(solution)/shard_map/ppermute | solution.py:28
  272.4 27.7 %collective-permute-start.1 = (bf16[512,512]{1,0:T(8,128)(2,1)}, bf16[512,512]{1,0:T(8,128)(2,1)S(1)}, u32[]{:S(2)}, u32[]{:S(2)}) collective-permute-start(bf16[512,512]{1,0:T(8,128)(2,1)} %collective-permute-done.refs_1_), channel_id=1, source_target_pairs={{0,2},{2,4},{4,6},{6,8},{8,10},{10,12},{12,14},{14,16},{16,18},{18... | collective-permute-start | bytes 1572872 | tf_op jit(solution)/shard_map/ppermute | solution.py:28
  300.1 21.5 %copy-start.27 = (s32[512]{0:T(512)S(1)}, s32[512]{0:T(512)}, u32[]{:S(2)}) copy-start(s32[512]{0:T(512)} %param.13) | copy-start | bytes 6148
  307.2 12.9 %collective-permute-start.8 = (bf16[512,512]{0,1:T(8,128)(2,1)}, bf16[512,512]{0,1:T(8,128)(2,1)}, u32[]{:S(2)}, u32[]{:S(2)}) collective-permute-start(bf16[512,512]{0,1:T(8,128)(2,1)} %fusion.20), channel_id=1, source_target_pairs={{0,1},{1,0},{2,3},{3,2},{4,5},{5,4},{6,7},{7,6},{8,9},{9,8},{10,11... | collective-permute-start | bytes 1572872 | tf_op jit(solution)/shard_map/ppermute | solution.py:32
  338.9 46.2 %collective-permute-start.15 = (bf16[512,512]{1,0:T(8,128)(2,1)}, bf16[512,512]{1,0:T(8,128)(2,1)S(1)}, u32[]{:S(2)}, u32[]{:S(2)}) collective-permute-start(bf16[512,512]{1,0:T(8,128)(2,1)} %get-tuple-element.47), channel_id=1, source_target_pairs={{2,0},{4,2},{6,4},{8,6},{10,8},{12,10},{14,12},{16,14},{18,16},{20... | collective-permute-start | bytes 1572872 | tf_op jit(solution)/shard_map/ppermute | solution.py:28
  354.4 41.1 %collective-permute-start.13 = (bf16[512,512]{1,0:T(8,128)(2,1)S(1)}, bf16[512,512]{1,0:T(8,128)(2,1)S(1)}, u32[]{:S(2)}, u32[]{:S(2)}) collective-permute-start(bf16[512,512]{1,0:T(8,128)(2,1)S(1)} %get-tuple-element.44), channel_id=1, source_target_pairs={{2,0},{4,2},{6,4},{8,6},{10,8},{12,10},{14,12},{16,14},{18,16},{20... | collective-permute-start | bytes 1572872 | tf_op jit(solution)/shard_map/ppermute | solution.py:28
  368.1 22.1 %collective-permute-start.9 = (bf16[512,512]{1,0:T(8,128)(2,1)S(1)}, bf16[512,512]{1,0:T(8,128)(2,1)}, u32[]{:S(2)}, u32[]{:S(2)}) collective-permute-start(bf16[512,512]{1,0:T(8,128)(2,1)S(1)} %get-tuple-element.38), channel_id=1, source_target_pairs={{2,0},{4,2},{6,4},{8,6},{10,8},{12,10},{14,12},{16,14},{18,16},{20... | collective-permute-start | bytes 1572872 | tf_op jit(solution)/shard_map/ppermute | solution.py:28
  381.8 22.8 %copy-start.3 = (f32[512,512]{1,0:T(8,128)S(1)}, f32[512,512]{1,0:T(8,128)}, u32[]{:S(2)}) copy-start(f32[512,512]{1,0:T(8,128)} %copy-done.2) | copy-start | bytes 3145732
  381.8 11.6 %collective-permute-start.11 = (bf16[512,512]{1,0:T(8,128)(2,1)S(1)}, bf16[512,512]{1,0:T(8,128)(2,1)S(1)}, u32[]{:S(2)}, u32[]{:S(2)}) collective-permute-start(bf16[512,512]{1,0:T(8,128)(2,1)S(1)} %get-tuple-element.41), channel_id=1, source_target_pairs={{2,0},{4,2},{6,4},{8,6},{10,8},{12,10},{14,12},{16,14},{18,16},{20... | collective-permute-start | bytes 1572872 | tf_op jit(solution)/shard_map/ppermute | solution.py:28
  387.1 37.9 %collective-permute-start.16 = (bf16[512,512]{1,0:T(8,128)(2,1)S(1)}, bf16[512,512]{1,0:T(8,128)(2,1)S(1)}, u32[]{:S(2)}, u32[]{:S(2)}) collective-permute-start(bf16[512,512]{1,0:T(8,128)(2,1)S(1)} %add_convert_fusion.2), channel_id=1, source_target_pairs={{2,0},{4,2},{6,4},{8,6},{10,8},{12,10},{14,12},{16,14},{18,16},{20... | collective-permute-start | bytes 1572872 | tf_op jit(solution)/shard_map/ppermute | solution.py:28
  391.4 13.1 %collective-permute-start.10 = (bf16[512,512]{1,0:T(8,128)(2,1)S(1)}, bf16[512,512]{1,0:T(8,128)(2,1)S(1)}, u32[]{:S(2)}, u32[]{:S(2)}) collective-permute-start(bf16[512,512]{1,0:T(8,128)(2,1)S(1)} %add_convert_fusion.5), channel_id=1, source_target_pairs={{2,0},{4,2},{6,4},{8,6},{10,8},{12,10},{14,12},{16,14},{18,16},{20... | collective-permute-start | bytes 1572872 | tf_op jit(solution)/shard_map/ppermute | solution.py:28
  393.5 17.8 %collective-permute-start.12 = (bf16[512,512]{1,0:T(8,128)(2,1)S(1)}, bf16[512,512]{1,0:T(8,128)(2,1)S(1)}, u32[]{:S(2)}, u32[]{:S(2)}) collective-permute-start(bf16[512,512]{1,0:T(8,128)(2,1)S(1)} %add_convert_fusion.4), channel_id=1, source_target_pairs={{2,0},{4,2},{6,4},{8,6},{10,8},{12,10},{14,12},{16,14},{18,16},{20... | collective-permute-start | bytes 1572872 | tf_op jit(solution)/shard_map/ppermute | solution.py:28
  395.7 22.3 %collective-permute-start.14 = (bf16[512,512]{1,0:T(8,128)(2,1)S(1)}, bf16[512,512]{1,0:T(8,128)(2,1)S(1)}, u32[]{:S(2)}, u32[]{:S(2)}) collective-permute-start(bf16[512,512]{1,0:T(8,128)(2,1)S(1)} %add_convert_fusion.3), channel_id=1, source_target_pairs={{2,0},{4,2},{6,4},{8,6},{10,8},{12,10},{14,12},{16,14},{18,16},{20... | collective-permute-start | bytes 1572872 | tf_op jit(solution)/shard_map/ppermute | solution.py:28
  434.2 61.9 %collective-permute-start.17 = (bf16[512,2688]{1,0:T(8,128)(2,1)}, bf16[512,2688]{1,0:T(8,128)(2,1)}, u32[]{:S(2)}, u32[]{:S(2)}) collective-permute-start(bf16[512,2688]{1,0:T(8,128)(2,1)} %add_convert_fusion), channel_id=1, source_target_pairs={{0,1},{1,0},{2,3},{3,2},{4,5},{5,4},{6,7},{7,6},{8,9},{9,8},{10,11... | collective-permute-start | bytes 8257544 | tf_op jit(solution)/shard_map/ppermute | solution.py:32
  (32 other events, 200.4 us)
Sparse Core Ops, SparseCore 0:
  10.9 58.0 all-gather.10
  71.2 59.1 all-gather.6
  133.3 59.5 all-gather.8
  195.0 58.1 all-gather.4

commit v2 on v1

--- a/solution.py
+++ b/solution.py
@@ -11,6 +11,7 @@
 WINDOW_KEYS = 1024
 TILE = 256
 GROUPS = 4
+COLUMNS = 384
 
 norm_eps = 1e-06
 softcap = 30.0
@@ -45,10 +46,19 @@
     return inverse * (upstream - unit * jnp.mean(unit * upstream, axis=-1, keepdims=True))
 
 
-def prep_kernel(raw_ref, kv_ref):
+def project_kernel(x_ref, w_ref, raw_ref, kv_ref):
+    raw_ref[...] = dot(x_ref[...], w_ref[...])
     unit, _ = normalized_rows(raw_ref[:, :HEAD_SIZE])
     kv_ref[:, :HEAD_SIZE] = unit.astype(jnp.bfloat16)
     kv_ref[:, HEAD_SIZE:] = raw_ref[:, HEAD_SIZE:].astype(jnp.bfloat16)
+
+
+def product_kernel(count, start_ref, *refs):
+    grads, weights, out_ref = refs[:count], refs[count : 2 * count], refs[2 * count]
+    total = dot(grads[0][...], weights[0][...], NT)
+    for n in range(1, count):
+        total += dot(grads[n][...], weights[n][...], NT)
+    out_ref[...] = total.astype(out_ref.dtype)
 
 
 def post_kernel(raw_ref, arrived_ref, own_ref, out_ref):
@@ -147,20 +157,53 @@
     return pl.BlockSpec((tokens, width), lambda h: (0, first + h))
 
 
-def prep(raw):
-    tokens, width = raw.shape
-    spec = columns(tokens, 2 * HEAD_SIZE)
-    return pl.pallas_call(
-        prep_kernel,
-        grid=(width // (2 * HEAD_SIZE),),
-        in_specs=[spec],
-        out_specs=spec,
-        out_shape=jax.ShapeDtypeStruct((tokens, width), jnp.bfloat16),
-        compiler_params=params(),
-        cost_estimate=pl.CostEstimate(
-            flops=6 * tokens * width, bytes_accessed=6 * tokens * width, transcendentals=0
-        ),
-    )(raw)
+def project(inputs, weight, first, heads):
+    tokens, model = inputs.shape
+    width = heads * 2 * HEAD_SIZE
+    return pl.pallas_call(
+        project_kernel,
+        grid=(heads,),
+        in_specs=[
+            pl.BlockSpec((tokens, model), lambda h: (0, 0)),
+            columns(model, 2 * HEAD_SIZE, first),
+        ],
+        out_specs=[columns(tokens, 2 * HEAD_SIZE)] * 2,
+        out_shape=[
+            jax.ShapeDtypeStruct((tokens, width), jnp.float32),
+            jax.ShapeDtypeStruct((tokens, width), jnp.bfloat16),
+        ],
+        compiler_params=params(),
+        cost_estimate=pl.CostEstimate(
+            flops=2 * tokens * width * model,
+            bytes_accessed=2 * model * (tokens + width) + 6 * tokens * width,
+            transcendentals=0,
+        ),
+    )(inputs, weight)
+
+
+def product(start, blocks, grads, weights):
+    tokens, width = grads[0].shape
+    count = len(grads)
+    specs = [pl.BlockSpec((tokens, width), lambda i, s: (0, 0))] * count
+    for _, at in weights:
+        specs.append(pl.BlockSpec((COLUMNS, width), lambda i, s, at=at: (s[0] + i, at)))
+    size = blocks * COLUMNS
+    return pl.pallas_call(
+        functools.partial(product_kernel, count),
+        grid_spec=pltpu.PrefetchScalarGridSpec(
+            num_scalar_prefetch=1,
+            grid=(blocks,),
+            in_specs=specs,
+            out_specs=pl.BlockSpec((tokens, COLUMNS), lambda i, s: (0, i)),
+        ),
+        out_shape=jax.ShapeDtypeStruct((tokens, size), jnp.bfloat16),
+        compiler_params=params(),
+        cost_estimate=pl.CostEstimate(
+            flops=2 * tokens * width * count * size,
+            bytes_accessed=2 * width * count * (tokens + size) + 2 * tokens * size,
+            transcendentals=0,
+        ),
+    )(jnp.reshape(start, (1,)).astype(jnp.int32), *grads, *[array for array, _ in weights])
 
 
 def post(raw, arrived, own):
@@ -245,16 +288,16 @@
     position = lax.axis_index("seq")
     valid = (position >= reach - jnp.arange(reach + 1)).astype(jnp.float32)
 
-    weights, raws, windows, outs, sums = [], [], [], [], []
+    parts = []
+    for h in range(kv_heads):
+        cols = slice(h * HEAD_SIZE, (h + 1) * HEAD_SIZE)
+        parts += [key_matrix[:, cols], value_matrix[:, cols]]
+    weight = lax.all_gather(jnp.concatenate(parts, axis=1), "seq", axis=0, tiled=True)
+
+    raws, windows, outs, sums = [], [], [], []
     partial = None
     for n in range(groups):
-        parts = []
-        for h in range(n * heads, (n + 1) * heads):
-            cols = slice(h * HEAD_SIZE, (h + 1) * HEAD_SIZE)
-            parts += [key_matrix[:, cols], value_matrix[:, cols]]
-        weight = lax.all_gather(jnp.concatenate(parts, axis=1), "seq", axis=0, tiled=True)
-        raw = dot(inputs, weight)
-        moving = prep(raw)
+        raw, moving = project(inputs, weight, n * heads, heads)
         window = [moving]
         for _ in range(reach):
             moving = passed_along(moving, "seq", 1)
@@ -262,7 +305,6 @@
         out, total = attention_forward(valid, queries, window, n * heads, heads, group)
         term = dot(out, readout[n * wide : (n + 1) * wide])
         partial = term if partial is None else partial + term
-        weights.append(weight)
         raws.append(raw)
         windows.append(window)
         outs.append(out)
@@ -295,22 +337,22 @@
             total = (arrived + pieces[slot]).astype(jnp.bfloat16)
         grads.append(post(raws[n], passed_along(total, "seq", -1), pieces[reach]))
 
-    def product(low, size):
-        result = None
-        for grad, weight in zip(grads, weights):
-            term = dot(grad, lax.dynamic_slice_in_dim(weight, low, size, 0), NT)
-            result = term if result is None else result + term
-        return result.astype(jnp.bfloat16)
-
-    model = weights[0].shape[0]
+    blocks = weight.shape[0] // COLUMNS
+    factors = [(weight, n) for n in range(groups)]
     if lax.axis_size("head") == 2:
-        half = model // 2
+        half = blocks // 2
         me = lax.axis_index("head")
-        arrived = swapped(product((1 - me) * half, half), "head")
-        input_grad = product(me * half, half).astype(jnp.float32) + arrived.astype(jnp.float32)
+        arrived = []
+        done = 0
+        for size in (half // 3, half // 3, half - 2 * (half // 3)):
+            term = product((1 - me) * half + done, size, grads, factors)
+            arrived.append(swapped(term, "head"))
+            done += size
+        own = product(me * half, half, grads, factors)
+        input_grad = own.astype(jnp.float32) + jnp.concatenate(arrived, axis=1).astype(jnp.float32)
     else:
         input_grad = lax.psum_scatter(
-            product(0, model), "head", scatter_dimension=1, tiled=True
+            product(0, blocks, grads, factors), "head", scatter_dimension=1, tiled=True
         ).astype(jnp.float32)
     return (jnp.concatenate(query_grads, axis=1), input_grad)
 

time: 521 us -> 406 us (0.78)
  waiting for transfers between devices: 264 us -> 178 us
  matrix products: 81.4 us -> 7.27 us
  Pallas kernels: 69.4 us -> 120 us
  other arithmetic: 23.4 us -> 10.1 us
  local copies, waits for them, and re-layouts: 11 us -> 21.9 us
    all_gather x4 -> x1, waiting for transfers between devices: 207 us -> 115 us  [shards(): lax.all_gather(jnp.concatenate(parts, axis=1), 'seq', axis=0, tiled=True)]
    dot_general x17 -> x5, matrix products: 81.4 us -> 7.27 us  [dot(): return lax.dot_general(a, b, dims, preferred_element_type=jnp.float32)]
    pallas_call x4 -> x8, Pallas kernels: 3.17 us -> 53.1 us  [the longest x4 28.9 us: project(): pl.pallas_call(project_kernel, grid=(heads,), in_specs=[pl.BlockSpec((tok...]
    unnamed x68 -> x77, local copies, waits for them, and re-layouts: 9.43 us -> 21.9 us
    add x1, other arithmetic: 11.7 us -> 4.25 us  [shards(): own.astype(jnp.float32)]
    ppermute x16, waiting for transfers between devices: 9.41 us -> 15.5 us  [passed_along(): lax.ppermute(value, axis, [(source, source + steps) for source in range(l...]
    ppermute x16, starting transfers between devices: 48.1 us -> 42.5 us  [passed_along(): lax.ppermute(value, axis, [(source, source + steps) for source in range(l...]
    ppermute x2 -> x4, waiting for transfers between devices: 47.6 us -> 47 us  [swapped(): return lax.ppermute(value, axis, [(0, 1), (1, 0)])]
  transfers between devices with their start and end apart: 22 -> 21, of which waited for: 8 -> 11; matrix products, arithmetic and copies ran while one was open for 15% -> 2% of each run, Pallas kernels for 10% -> 23%
where the time goes in v2:
time: 406 us; the launch traced here: 399 us
  waiting for transfers between devices  178 us (44%)
  Pallas kernels  120 us (30%)
  starting transfers between devices  46.7 us (12%)
  local copies, waits for them, and re-layouts  21.9 us (5%)
  between operations  15.2 us (4%)
  other arithmetic  10.1 us (2%)
  matrix products  7.27 us (2%)
    all_gather x1, waiting for transfers between devices, shards(): lax.all_gather(jnp.concatenate(parts, axis=1), 'seq', axis=0, tiled=True)  115 us
    ppermute x4, waiting for transfers between devices, swapped(): return lax.ppermute(value, axis, [(0, 1), (1, 0)])  47 us
    ppermute x16, starting transfers between devices, passed_along(): lax.ppermute(value, axis, [(source, source + steps) for source in range(l...  42.5 us
    pallas_call x4, Pallas kernels, attention_backward(): pl.pallas_call(functools.partial(backward_kernel, reach, group), grid=(he...  42.5 us
    pallas_call x4, Pallas kernels, project(): pl.pallas_call(project_kernel, grid=(heads,), in_specs=[pl.BlockSpec((tok...  28.9 us
    pallas_call x4, Pallas kernels, product(): pl.pallas_call(functools.partial(product_kernel, count), grid_spec=pltpu....  24.2 us
    unnamed x77, local copies, waits for them, and re-layouts  21.9 us
    pallas_call x4, Pallas kernels, attention_forward(): pl.pallas_call(functools.partial(forward_kernel, reach, group), grid=(hea...  19.1 us
  transfers between devices with their start and end apart: 21, of which 11 were waited for; matrix products, arithmetic and copies ran while one was open for 2% of the time, Pallas kernels for 23%

profile of v2, /device:TPU:13, one launch (start us, length us, event | category | flops | bytes accessed | tf_op | source)
XLA Modules:
  0.0 399.3 jit_solution(17466998958162088668)
XLA Ops:
  16.1 115.2 %all-gather.2.cloned.1.call-done.w_ref.refs_4_.refs_5_.refs_6_.refs_7_ = bf16[5376,2048]{1,0:T(8,128)(2,1)} async-done(((bf16[336,2048]{1,0:T(8,128)(2,1)}), bf16[5376,2048]{1,0:T(8,128)(2,1)}) %all-gather.2.cloned.1.call-update) | async-done | bytes 22020112 | tf_op jit(solution)/shard_map/all_gather | solution.py:295
  131.4 6.9 %shard_map.86 = (f32[512,512]{1,0:T(8,128)S(1)}, bf16[512,512]{1,0:T(8,128)(2,1)S(1)}) custom-call(bf16[512,5376]{1,0:T(8,128)(2,1)} %x_ref.7, bf16[5376,2048]{1,0:T(8,128)(2,1)} %all-gather.2.cloned.1.call-done.w_ref.refs_4_.refs_5_.refs_6_.refs_7_), custom_call_target="tpu_custom_call" | custom-call | flops 2818572288 | bytes 12582912 | tf_op jit(solution)/shard_map/pallas_call | solution.py:163
  141.7 6.9 %shard_map.88 = (f32[512,512]{1,0:T(8,128)S(1)}, bf16[512,512]{1,0:T(8,128)(2,1)S(1)}) custom-call(bf16[512,5376]{1,0:T(8,128)(2,1)} %x_ref.7, bf16[5376,2048]{1,0:T(8,128)(2,1)} %all-gather.2.cloned.1.call-done.w_ref.refs_4_.refs_5_.refs_6_.refs_7_), custom_call_target="tpu_custom_call" | custom-call | flops 2818572288 | bytes 12582912 | tf_op jit(solution)/shard_map/pallas_call | solution.py:163
  151.8 7.6 %shard_map.90 = (f32[512,512]{1,0:T(8,128)S(1)}, bf16[512,512]{1,0:T(8,128)(2,1)}) custom-call(bf16[512,5376]{1,0:T(8,128)(2,1)} %x_ref.7, bf16[5376,2048]{1,0:T(8,128)(2,1)} %all-gather.2.cloned.1.call-done.w_ref.refs_4_.refs_5_.refs_6_.refs_7_), custom_call_target="tpu_custom_call" | custom-call | flops 2818572288 | bytes 12582912 | tf_op jit(solution)/shard_map/pallas_call | solution.py:163
  162.4 7.6 %shard_map.92 = (f32[512,512]{1,0:T(8,128)S(1)}, bf16[512,512]{1,0:T(8,128)(2,1)}) custom-call(bf16[512,5376]{1,0:T(8,128)(2,1)} %x_ref.7, bf16[5376,2048]{1,0:T(8,128)(2,1)} %all-gather.2.cloned.1.call-done.w_ref.refs_4_.refs_5_.refs_6_.refs_7_), custom_call_target="tpu_custom_call" | custom-call | flops 2818572288 | bytes 12582912 | tf_op jit(solution)/shard_map/pallas_call | solution.py:163
  187.7 4.8 %shard_map.89 = (bf16[512,512]{1,0:T(8,128)(2,1)S(1)}, f32[16,1024]{1,0:T(8,128)S(1)}) custom-call(f32[3]{0:T(128)S(1)} %compare_convert_fusion.valid_ref, bf16[512,2048]{1,0:T(8,128)(2,1)S(1)} %copy-done.20, bf16[512,512]{1,0:T(8,128)(2,1)} %collective-permute-done.3.refs_0_, bf16[512,512]{1,0:T(8,128)(2,1)} %collective-permute-done.2.refs_1_, ...), custom_call_target="tpu_custom_call" | custom-call | flops 2684354560 | bytes 2621440 | tf_op jit(solution)/shard_map/pallas_call | solution.py:230
  196.3 4.9 %shard_map.91 = (bf16[512,512]{1,0:T(8,128)(2,1)S(1)}, f32[16,1024]{1,0:T(8,128)S(1)}) custom-call(f32[3]{0:T(128)S(1)} %compare_convert_fusion.valid_ref, bf16[512,2048]{1,0:T(8,128)(2,1)S(1)} %copy-done.20, bf16[512,512]{1,0:T(8,128)(2,1)S(1)} %collective-permute-done.5.refs_0_, bf16[512,512]{1,0:T(8,128)(2,1)} %collective-permute-done.4.refs_1_, ...), custom_call_target="tpu_custom_call" | custom-call | flops 2684354560 | bytes 2621440 | tf_op jit(solution)/shard_map/pallas_call | solution.py:230
  203.0 5.0 %shard_map.93 = (bf16[512,512]{1,0:T(8,128)(2,1)S(1)}, f32[16,1024]{1,0:T(8,128)S(1)}) custom-call(f32[3]{0:T(128)S(1)} %compare_convert_fusion.valid_ref, bf16[512,2048]{1,0:T(8,128)(2,1)S(1)} %copy-done.21, bf16[512,512]{1,0:T(8,128)(2,1)S(1)} %collective-permute-done.7.refs_0_, bf16[512,512]{1,0:T(8,128)(2,1)} %collective-permute-done.6.refs_1_, ...), custom_call_target="tpu_custom_call" | custom-call | flops 2684354560 | bytes 2621440 | tf_op jit(solution)/shard_map/pallas_call | solution.py:230
  208.5 4.4 %shard_map.87 = (bf16[512,512]{1,0:T(8,128)(2,1)S(1)}, f32[16,1024]{1,0:T(8,128)S(1)}) custom-call(f32[3]{0:T(128)S(1)} %compare_convert_fusion.valid_ref, bf16[512,2048]{1,0:T(8,128)(2,1)S(1)} %copy-done.21, bf16[512,512]{1,0:T(8,128)(2,1)S(1)} %collective-permute-done.1.refs_0_, bf16[512,512]{1,0:T(8,128)(2,1)S(1)} %collective-permute-done.refs_1_, ...), custom_call_target="tpu_custom_call" | custom-call | flops 2684354560 | bytes 2621440 | tf_op jit(solution)/shard_map/pallas_call | solution.py:230
  214.7 10.7 %collective-permute-done.8 = bf16[512,512]{0,1:T(8,128)(2,1)S(1)} collective-permute-done((bf16[512,512]{0,1:T(8,128)(2,1)S(1)}, bf16[512,512]{0,1:T(8,128)(2,1)S(1)}, u32[]{:S(2)}, u32[]{:S(2)}) %collective-permute-start.8) | collective-permute-done | bytes 524320 | tf_op jit(solution)/shard_map/ppermute | solution.py:33
  228.8 10.7 %shard_map.97 = (f32[512,512]{1,0:T(8,128)S(1)}, bf16[512,512]{1,0:T(8,128)(2,1)S(1)}, f32[512,512]{1,0:T(8,128)S(1)}, f32[512,512]{1,0:T(8,128)S(1)}) custom-call(f32[3]{0:T(128)S(1)} %compare_convert_fusion.valid_ref, bf16[512,2048]{1,0:T(8,128)(2,1)} %q_ref.15, bf16[512,512]{1,0:T(8,128)(2,1)S(1)} %get-tuple-element.41.o_ref, ...), custom_call_target="tpu_custom_call" | custom-call | flops 5368709120 | bytes 6291456 | tf_op jit(solution)/shard_map/pallas_call | solution.py:256
  241.5 4.4 %collective-permute-start.15 = (bf16[512,512]{1,0:T(8,128)(2,1)S(1)}, bf16[512,512]{1,0:T(8,128)(2,1)S(1)}, u32[]{:S(2)}, u32[]{:S(2)}) collective-permute-start(bf16[512,512]{1,0:T(8,128)(2,1)S(1)} %get-tuple-element.63), channel_id=1, source_target_pairs={{2,0},{4,2},{6,4},{8,6},{10,8},{12,10},{14,12},{16,14},{18,16},{20... | collective-permute-start | bytes 1572872 | tf_op jit(solution)/shard_map/ppermute | solution.py:29
  245.8 10.6 %shard_map.96 = (f32[512,512]{1,0:T(8,128)S(1)}, bf16[512,512]{1,0:T(8,128)(2,1)S(1)}, f32[512,512]{1,0:T(8,128)S(1)}, f32[512,512]{1,0:T(8,128)S(1)}) custom-call(f32[3]{0:T(128)S(1)} %compare_convert_fusion.valid_ref, bf16[512,2048]{1,0:T(8,128)(2,1)} %q_ref.15, bf16[512,512]{1,0:T(8,128)(2,1)S(1)} %get-tuple-element.39.o_ref, ...), custom_call_target="tpu_custom_call" | custom-call | flops 5368709120 | bytes 6291456 | tf_op jit(solution)/shard_map/pallas_call | solution.py:256
  260.4 10.8 %shard_map.95 = (f32[512,512]{1,0:T(8,128)S(1)}, bf16[512,512]{1,0:T(8,128)(2,1)S(1)}, f32[512,512]{1,0:T(8,128)S(1)}, f32[512,512]{1,0:T(8,128)S(1)}) custom-call(f32[3]{0:T(128)S(1)} %compare_convert_fusion.valid_ref, bf16[512,2048]{1,0:T(8,128)(2,1)} %q_ref.15, bf16[512,512]{1,0:T(8,128)(2,1)S(1)} %get-tuple-element.37.o_ref, ...), custom_call_target="tpu_custom_call" | custom-call | flops 5368709120 | bytes 6291456 | tf_op jit(solution)/shard_map/pallas_call | solution.py:256
  276.1 10.3 %shard_map.94 = (f32[512,512]{1,0:T(8,128)S(1)}, bf16[512,512]{1,0:T(8,128)(2,1)S(1)}, f32[512,512]{1,0:T(8,128)S(1)}, f32[512,512]{1,0:T(8,128)S(1)}) custom-call(f32[3]{0:T(128)S(1)} %compare_convert_fusion.valid_ref, bf16[512,2048]{1,0:T(8,128)(2,1)} %q_ref.15, bf16[512,512]{1,0:T(8,128)(2,1)S(1)} %get-tuple-element.35.o_ref, ...), custom_call_target="tpu_custom_call" | custom-call | flops 5368709120 | bytes 6291456 | tf_op jit(solution)/shard_map/pallas_call | solution.py:256
  310.9 4.0 collective-permute-done.12.arrived_ref
  316.4 4.0 %collective-permute-done.10.arrived_ref = bf16[512,512]{1,0:T(8,128)(2,1)} collective-permute-done((bf16[512,512]{1,0:T(8,128)(2,1)}, bf16[512,512]{1,0:T(8,128)(2,1)}, u32[]{:S(2)}, u32[]{:S(2)}) %collective-permute-start.10) | collective-permute-done | bytes 524320 | tf_op jit(solution)/shard_map/ppermute | solution.py:29
  321.9 5.4 %shard_map.105 = bf16[512,1152]{1,0:T(8,128)(2,1)S(1)} custom-call(s32[1]{0:T(128)} %bitcast.3.start_ref, bf16[512,512]{1,0:T(8,128)(2,1)S(1)} %shard_map.98.refs_0_, bf16[512,512]{1,0:T(8,128)(2,1)S(1)} %shard_map.99.refs_1_, bf16[512,512]{1,0:T(8,128)(2,1)S(1)} %shard_map.100.refs_2_, bf16[512,512]{1,0:T(8,128)(2,1)S(1)} %shard_map.101.refs_3_, ...), custom_call_target="tpu_custom_call" | custom-call | flops 2415919104 | bytes 7995392 | tf_op jit(solution)/shard_map/pallas_call | solution.py:191
  328.6 4.0 %shard_map.103 = bf16[512,768]{1,0:T(8,128)(2,1)S(1)} custom-call(s32[1]{0:T(128)} %bitcast.1.start_ref, bf16[512,512]{1,0:T(8,128)(2,1)S(1)} %shard_map.98.refs_0_, bf16[512,512]{1,0:T(8,128)(2,1)S(1)} %shard_map.99.refs_1_, bf16[512,512]{1,0:T(8,128)(2,1)S(1)} %shard_map.100.refs_2_, bf16[512,512]{1,0:T(8,128)(2,1)S(1)} %shard_map.101.refs_3_, ...), custom_call_target="tpu_custom_call" | custom-call | flops 1610612736 | bytes 6029312 | tf_op jit(solution)/shard_map/pallas_call | solution.py:191
  332.9 4.2 %shard_map.104 = bf16[512,768]{1,0:T(8,128)(2,1)S(1)} custom-call(s32[1]{0:T(128)} %bitcast.2.start_ref, bf16[512,512]{1,0:T(8,128)(2,1)S(1)} %shard_map.98.refs_0_, bf16[512,512]{1,0:T(8,128)(2,1)S(1)} %shard_map.99.refs_1_, bf16[512,512]{1,0:T(8,128)(2,1)S(1)} %shard_map.100.refs_2_, bf16[512,512]{1,0:T(8,128)(2,1)S(1)} %shard_map.101.refs_3_, ...), custom_call_target="tpu_custom_call" | custom-call | flops 1610612736 | bytes 6029312 | tf_op jit(solution)/shard_map/pallas_call | solution.py:191
  340.8 10.6 %shard_map.102 = bf16[512,2688]{1,0:T(8,128)(2,1)S(1)} custom-call(s32[1]{0:T(128)} %bitcast.start_ref, bf16[512,512]{1,0:T(8,128)(2,1)S(1)} %shard_map.98.refs_0_, bf16[512,512]{1,0:T(8,128)(2,1)S(1)} %shard_map.99.refs_1_, bf16[512,512]{1,0:T(8,128)(2,1)S(1)} %shard_map.100.refs_2_, bf16[512,512]{1,0:T(8,128)(2,1)S(1)} %shard_map.101.refs_3_, ...), custom_call_target="tpu_custom_call" | custom-call | flops 5637144576 | bytes 15859712 | tf_op jit(solution)/shard_map/pallas_call | solution.py:191
  351.4 20.8 %collective-permute-done.17 = bf16[512,768]{1,0:T(8,128)(2,1)S(1)} collective-permute-done((bf16[512,768]{1,0:T(8,128)(2,1)S(1)}, bf16[512,768]{1,0:T(8,128)(2,1)S(1)}, u32[]{:S(2)}, u32[]{:S(2)}) %collective-permute-start.17) | collective-permute-done | bytes 786464 | tf_op jit(solution)/shard_map/ppermute | solution.py:33
  372.2 15.5 %collective-permute-done.18 = bf16[512,768]{1,0:T(8,128)(2,1)S(1)} collective-permute-done((bf16[512,768]{1,0:T(8,128)(2,1)S(1)}, bf16[512,768]{1,0:T(8,128)(2,1)S(1)}, u32[]{:S(2)}, u32[]{:S(2)}) %collective-permute-start.18) | collective-permute-done | bytes 786464 | tf_op jit(solution)/shard_map/ppermute | solution.py:33
  387.7 4.2 %convert_add_fusion = f32[512,2688]{1,0:T(8,128)} fusion(bf16[512,2688]{1,0:T(8,128)(2,1)S(1)} %shard_map.102, bf16[512,1152]{1,0:T(8,128)(2,1)} %collective-permute-done.19, bf16[512,768]{1,0:T(8,128)(2,1)S(1)} %collective-permute-done.18, bf16[512,768]{1,0:T(8,128)(2,1)S(1)} %collective-permute-done.17), kind=kLoop, calls=%fused_computation | loop fusion | flops 11010048 | bytes 11010048 | tf_op jit(solution)/shard_map/add | solution.py:352
  (131 shorter events, 90.7 us)
Async XLA Ops:
  7.2 124.2 %all-gather.2.cloned.1.call-start = ((), (), s32[]{:S(2)}) async-start(), calls=%async_computation | async-start | bytes 23396352 | tf_op jit(solution)/shard_map/all_gather | solution.py:295
  138.2 38.3 %collective-permute-start = (bf16[512,512]{1,0:T(8,128)(2,1)S(1)}, bf16[512,512]{1,0:T(8,128)(2,1)S(1)}, u32[]{:S(2)}, u32[]{:S(2)}) collective-permute-start(bf16[512,512]{1,0:T(8,128)(2,1)S(1)} %get-tuple-element.34.refs_2_), channel_id=1, source_target_pairs={{0,2},{2,4},{4,6},{6,8},{8,10},{10,12},{12,14},{14,16},{16,18},{18... | collective-permute-start | bytes 1572872 | tf_op jit(solution)/shard_map/ppermute | solution.py:29
  149.6 9.7 %copy-start.22 = (bf16[512,512]{1,0:T(8,128)(2,1)}, bf16[512,512]{1,0:T(8,128)(2,1)S(1)}, u32[]{:S(2)}) copy-start(bf16[512,512]{1,0:T(8,128)(2,1)S(1)} %get-tuple-element.36.refs_2_) | copy-start | bytes 1572868
  149.6 23.4 %collective-permute-start.2 = (bf16[512,512]{1,0:T(8,128)(2,1)S(1)}, bf16[512,512]{1,0:T(8,128)(2,1)}, u32[]{:S(2)}, u32[]{:S(2)}) collective-permute-start(bf16[512,512]{1,0:T(8,128)(2,1)S(1)} %get-tuple-element.36.refs_2_), channel_id=1, source_target_pairs={{0,2},{2,4},{4,6},{6,8},{8,10},{10,12},{12,14},{14,16},{16,18},{18... | collective-permute-start | bytes 1572872 | tf_op jit(solution)/shard_map/ppermute | solution.py:29
  159.4 19.4 %collective-permute-start.4 = (bf16[512,512]{1,0:T(8,128)(2,1)}, bf16[512,512]{1,0:T(8,128)(2,1)}, u32[]{:S(2)}, u32[]{:S(2)}) collective-permute-start(bf16[512,512]{1,0:T(8,128)(2,1)} %get-tuple-element.38.refs_2_), channel_id=1, source_target_pairs={{0,2},{2,4},{4,6},{6,8},{8,10},{10,12},{12,14},{14,16},{16,18},{18... | collective-permute-start | bytes 1572872 | tf_op jit(solution)/shard_map/ppermute | solution.py:29
  170.9 10.2 %collective-permute-start.6 = (bf16[512,512]{1,0:T(8,128)(2,1)}, bf16[512,512]{1,0:T(8,128)(2,1)}, u32[]{:S(2)}, u32[]{:S(2)}) collective-permute-start(bf16[512,512]{1,0:T(8,128)(2,1)} %get-tuple-element.40.refs_2_), channel_id=1, source_target_pairs={{0,2},{2,4},{4,6},{6,8},{8,10},{10,12},{12,14},{14,16},{16,18},{18... | collective-permute-start | bytes 1572872 | tf_op jit(solution)/shard_map/ppermute | solution.py:29
  173.1 12.0 %collective-permute-start.3 = (bf16[512,512]{1,0:T(8,128)(2,1)}, bf16[512,512]{1,0:T(8,128)(2,1)}, u32[]{:S(2)}, u32[]{:S(2)}) collective-permute-start(bf16[512,512]{1,0:T(8,128)(2,1)} %collective-permute-done.2.refs_1_), channel_id=1, source_target_pairs={{0,2},{2,4},{4,6},{6,8},{8,10},{10,12},{12,14},{14,16},{16,18},{18... | collective-permute-start | bytes 1572872 | tf_op jit(solution)/shard_map/ppermute | solution.py:29
  176.6 31.9 %collective-permute-start.1 = (bf16[512,512]{1,0:T(8,128)(2,1)S(1)}, bf16[512,512]{1,0:T(8,128)(2,1)S(1)}, u32[]{:S(2)}, u32[]{:S(2)}) collective-permute-start(bf16[512,512]{1,0:T(8,128)(2,1)S(1)} %collective-permute-done.refs_1_), channel_id=1, source_target_pairs={{0,2},{2,4},{4,6},{6,8},{8,10},{10,12},{12,14},{14,16},{16,18},{18... | collective-permute-start | bytes 1572872 | tf_op jit(solution)/shard_map/ppermute | solution.py:29
  178.8 17.6 %collective-permute-start.5 = (bf16[512,512]{1,0:T(8,128)(2,1)}, bf16[512,512]{1,0:T(8,128)(2,1)S(1)}, u32[]{:S(2)}, u32[]{:S(2)}) collective-permute-start(bf16[512,512]{1,0:T(8,128)(2,1)} %collective-permute-done.4.refs_1_), channel_id=1, source_target_pairs={{0,2},{2,4},{4,6},{6,8},{8,10},{10,12},{12,14},{14,16},{16,18},{18... | collective-permute-start | bytes 1572872 | tf_op jit(solution)/shard_map/ppermute | solution.py:29
  181.1 21.8 %collective-permute-start.7 = (bf16[512,512]{1,0:T(8,128)(2,1)}, bf16[512,512]{1,0:T(8,128)(2,1)S(1)}, u32[]{:S(2)}, u32[]{:S(2)}) collective-permute-start(bf16[512,512]{1,0:T(8,128)(2,1)} %collective-permute-done.6.refs_1_), channel_id=1, source_target_pairs={{0,2},{2,4},{4,6},{6,8},{8,10},{10,12},{12,14},{14,16},{16,18},{18... | collective-permute-start | bytes 1572872 | tf_op jit(solution)/shard_map/ppermute | solution.py:29
  212.9 12.8 %copy-start.30 = (s32[512]{0:T(512)S(1)}, s32[512]{0:T(512)}, u32[]{:S(2)}) copy-start(s32[512]{0:T(512)} %param.13) | copy-start | bytes 6148
  213.4 11.9 %collective-permute-start.8 = (bf16[512,512]{0,1:T(8,128)(2,1)S(1)}, bf16[512,512]{0,1:T(8,128)(2,1)S(1)}, u32[]{:S(2)}, u32[]{:S(2)}) collective-permute-start(bf16[512,512]{0,1:T(8,128)(2,1)S(1)} %fusion.2), channel_id=1, source_target_pairs={{0,1},{1,0},{2,3},{3,2},{4,5},{5,4},{6,7},{7,6},{8,9},{9,8},{10,11... | collective-permute-start | bytes 1572872 | tf_op jit(solution)/shard_map/ppermute | solution.py:33
  241.5 47.0 %collective-permute-start.15 = (bf16[512,512]{1,0:T(8,128)(2,1)S(1)}, bf16[512,512]{1,0:T(8,128)(2,1)S(1)}, u32[]{:S(2)}, u32[]{:S(2)}) collective-permute-start(bf16[512,512]{1,0:T(8,128)(2,1)S(1)} %get-tuple-element.63), channel_id=1, source_target_pairs={{2,0},{4,2},{6,4},{8,6},{10,8},{12,10},{14,12},{16,14},{18,16},{20... | collective-permute-start | bytes 1572872 | tf_op jit(solution)/shard_map/ppermute | solution.py:29
  245.8 14.6 %copy-start.24 = (bf16[512,512]{1,0:T(8,128)(2,1)S(1)}, bf16[512,512]{1,0:T(8,128)(2,1)}, u32[]{:S(2)}) copy-start(bf16[512,512]{1,0:T(8,128)(2,1)} %copy-done.22) | copy-start | bytes 1572868
  258.5 33.3 %collective-permute-start.13 = (bf16[512,512]{1,0:T(8,128)(2,1)S(1)}, bf16[512,512]{1,0:T(8,128)(2,1)S(1)}, u32[]{:S(2)}, u32[]{:S(2)}) collective-permute-start(bf16[512,512]{1,0:T(8,128)(2,1)S(1)} %get-tuple-element.59), channel_id=1, source_target_pairs={{2,0},{4,2},{6,4},{8,6},{10,8},{12,10},{14,12},{16,14},{18,16},{20... | collective-permute-start | bytes 1572872 | tf_op jit(solution)/shard_map/ppermute | solution.py:29
  273.3 21.5 %collective-permute-start.11 = (bf16[512,512]{1,0:T(8,128)(2,1)S(1)}, bf16[512,512]{1,0:T(8,128)(2,1)S(1)}, u32[]{:S(2)}, u32[]{:S(2)}) collective-permute-start(bf16[512,512]{1,0:T(8,128)(2,1)S(1)} %get-tuple-element.55), channel_id=1, source_target_pairs={{2,0},{4,2},{6,4},{8,6},{10,8},{12,10},{14,12},{16,14},{18,16},{20... | collective-permute-start | bytes 1572872 | tf_op jit(solution)/shard_map/ppermute | solution.py:29
  286.4 11.4 %collective-permute-start.9 = (bf16[512,512]{1,0:T(8,128)(2,1)S(1)}, bf16[512,512]{1,0:T(8,128)(2,1)S(1)}, u32[]{:S(2)}, u32[]{:S(2)}) collective-permute-start(bf16[512,512]{1,0:T(8,128)(2,1)S(1)} %get-tuple-element.51), channel_id=1, source_target_pairs={{2,0},{4,2},{6,4},{8,6},{10,8},{12,10},{14,12},{16,14},{18,16},{20... | collective-permute-start | bytes 1572872 | tf_op jit(solution)/shard_map/ppermute | solution.py:29
  288.6 14.9 %collective-permute-start.16 = (bf16[512,512]{1,0:T(8,128)(2,1)S(1)}, bf16[512,512]{1,0:T(8,128)(2,1)S(1)}, u32[]{:S(2)}, u32[]{:S(2)}) collective-permute-start(bf16[512,512]{1,0:T(8,128)(2,1)S(1)} %add_convert_fusion), channel_id=1, source_target_pairs={{2,0},{4,2},{6,4},{8,6},{10,8},{12,10},{14,12},{16,14},{18,16},{20... | collective-permute-start | bytes 1572872 | tf_op jit(solution)/shard_map/ppermute | solution.py:29
  292.8 16.4 %collective-permute-start.14 = (bf16[512,512]{1,0:T(8,128)(2,1)}, bf16[512,512]{1,0:T(8,128)(2,1)}, u32[]{:S(2)}, u32[]{:S(2)}) collective-permute-start(bf16[512,512]{1,0:T(8,128)(2,1)} %add_convert_fusion.1), channel_id=1, source_target_pairs={{2,0},{4,2},{6,4},{8,6},{10,8},{12,10},{14,12},{16,14},{18,16},{20... | collective-permute-start | bytes 1572872 | tf_op jit(solution)/shard_map/ppermute | solution.py:29
  295.7 19.1 %collective-permute-start.12 = (bf16[512,512]{1,0:T(8,128)(2,1)}, bf16[512,512]{1,0:T(8,128)(2,1)}, u32[]{:S(2)}, u32[]{:S(2)}) collective-permute-start(bf16[512,512]{1,0:T(8,128)(2,1)} %add_convert_fusion.2), channel_id=1, source_target_pairs={{2,0},{4,2},{6,4},{8,6},{10,8},{12,10},{14,12},{16,14},{18,16},{20... | collective-permute-start | bytes 1572872 | tf_op jit(solution)/shard_map/ppermute | solution.py:29
  298.8 21.6 %collective-permute-start.10 = (bf16[512,512]{1,0:T(8,128)(2,1)}, bf16[512,512]{1,0:T(8,128)(2,1)}, u32[]{:S(2)}, u32[]{:S(2)}) collective-permute-start(bf16[512,512]{1,0:T(8,128)(2,1)} %add_convert_fusion.3), channel_id=1, source_target_pairs={{2,0},{4,2},{6,4},{8,6},{10,8},{12,10},{14,12},{16,14},{18,16},{20... | collective-permute-start | bytes 1572872 | tf_op jit(solution)/shard_map/ppermute | solution.py:29
  327.3 60.4 %collective-permute-start.19 = (bf16[512,1152]{1,0:T(8,128)(2,1)S(1)}, bf16[512,1152]{1,0:T(8,128)(2,1)}, u32[]{:S(2)}, u32[]{:S(2)}) collective-permute-start(bf16[512,1152]{1,0:T(8,128)(2,1)S(1)} %shard_map.105), channel_id=1, source_target_pairs={{0,1},{1,0},{2,3},{3,2},{4,5},{5,4},{6,7},{7,6},{8,9},{9,8},{10,11... | collective-permute-start | bytes 3538952 | tf_op jit(solution)/shard_map/ppermute | solution.py:33
  332.6 39.6 %collective-permute-start.17 = (bf16[512,768]{1,0:T(8,128)(2,1)S(1)}, bf16[512,768]{1,0:T(8,128)(2,1)S(1)}, u32[]{:S(2)}, u32[]{:S(2)}) collective-permute-start(bf16[512,768]{1,0:T(8,128)(2,1)S(1)} %shard_map.103), channel_id=1, source_target_pairs={{0,1},{1,0},{2,3},{3,2},{4,5},{5,4},{6,7},{7,6},{8,9},{9,8},{10,11... | collective-permute-start | bytes 2359304 | tf_op jit(solution)/shard_map/ppermute | solution.py:33
  337.1 50.6 %collective-permute-start.18 = (bf16[512,768]{1,0:T(8,128)(2,1)S(1)}, bf16[512,768]{1,0:T(8,128)(2,1)S(1)}, u32[]{:S(2)}, u32[]{:S(2)}) collective-permute-start(bf16[512,768]{1,0:T(8,128)(2,1)S(1)} %shard_map.104), channel_id=1, source_target_pairs={{0,1},{1,0},{2,3},{3,2},{4,5},{5,4},{6,7},{7,6},{8,9},{9,8},{10,11... | collective-permute-start | bytes 2359304 | tf_op jit(solution)/shard_map/ppermute | solution.py:33
  (28 other events, 92.5 us)
Sparse Core Ops, SparseCore 0:
  16.2 115.0 all-gather.1

commit v3 on v2

--- a/solution.py
+++ b/solution.py
@@ -10,7 +10,8 @@
 HEAD_SIZE = 128
 WINDOW_KEYS = 1024
 TILE = 256
-GROUPS = 4
+FORWARD_GROUPS = 2
+BACKWARD_GROUPS = 4
 COLUMNS = 384
 
 norm_eps = 1e-06
@@ -51,6 +52,14 @@
     unit, _ = normalized_rows(raw_ref[:, :HEAD_SIZE])
     kv_ref[:, :HEAD_SIZE] = unit.astype(jnp.bfloat16)
     kv_ref[:, HEAD_SIZE:] = raw_ref[:, HEAD_SIZE:].astype(jnp.bfloat16)
+
+
+def interleave_kernel(k_ref, v_ref, out_ref):
+    for h in range(k_ref.shape[1] // HEAD_SIZE):
+        cols = slice(h * HEAD_SIZE, (h + 1) * HEAD_SIZE)
+        low = 2 * h * HEAD_SIZE
+        out_ref[:, low : low + HEAD_SIZE] = k_ref[:, cols]
+        out_ref[:, low + HEAD_SIZE : low + 2 * HEAD_SIZE] = v_ref[:, cols]
 
 
 def product_kernel(count, start_ref, *refs):
@@ -157,6 +166,15 @@
     return pl.BlockSpec((tokens, width), lambda h: (0, first + h))
 
 
+def interleave(keys, values):
+    rows, width = keys.shape
+    return pl.pallas_call(
+        interleave_kernel,
+        out_shape=jax.ShapeDtypeStruct((rows, 2 * width), keys.dtype),
+        compiler_params=params(),
+    )(keys, values)
+
+
 def project(inputs, weight, first, heads):
     tokens, model = inputs.shape
     width = heads * 2 * HEAD_SIZE
@@ -206,13 +224,13 @@
     )(jnp.reshape(start, (1,)).astype(jnp.int32), *grads, *[array for array, _ in weights])
 
 
-def post(raw, arrived, own):
-    tokens, width = raw.shape
+def post(raw, arrived, own, first):
+    tokens, width = own.shape
     spec = columns(tokens, 2 * HEAD_SIZE)
     return pl.pallas_call(
         post_kernel,
         grid=(width // (2 * HEAD_SIZE),),
-        in_specs=[spec] * 3,
+        in_specs=[columns(tokens, 2 * HEAD_SIZE, first), spec, spec],
         out_specs=spec,
         out_shape=jax.ShapeDtypeStruct((tokens, width), jnp.bfloat16),
         compiler_params=params(),
@@ -247,7 +265,7 @@
     )(valid, queries, *window)
 
 
-def attention_backward(valid, queries, attended, grad, sums, window, first, heads, group):
+def attention_backward(valid, queries, attended, grad, sums, window, first, inner, heads, group):
     tokens = queries.shape[0]
     reach = len(window) - 1
     wide = group * HEAD_SIZE
@@ -259,11 +277,11 @@
         in_specs=[
             pl.BlockSpec(memory_space=pltpu.SMEM),
             columns(tokens, wide, first),
-            columns(tokens, wide),
+            columns(tokens, wide, inner),
             columns(tokens, wide, first),
-            pl.BlockSpec((8, group * tokens), lambda h: (h, 0)),
+            pl.BlockSpec((8, group * tokens), lambda h: (inner + h, 0)),
         ]
-        + [columns(tokens, 2 * HEAD_SIZE)] * (reach + 1),
+        + [columns(tokens, 2 * HEAD_SIZE, inner)] * (reach + 1),
         out_specs=[columns(tokens, wide)] + [columns(tokens, 2 * HEAD_SIZE)] * (reach + 1),
         out_shape=[jax.ShapeDtypeStruct((tokens, heads * wide), jnp.float32)]
         + [jax.ShapeDtypeStruct((tokens, heads * 2 * HEAD_SIZE), kind) for kind in kinds],
@@ -282,17 +300,13 @@
     q_heads = queries.shape[1] // HEAD_SIZE
     group = q_heads // kv_heads
     reach = WINDOW_KEYS // tokens
-    groups = min(GROUPS, kv_heads)
+    groups = min(FORWARD_GROUPS, kv_heads)
     heads = kv_heads // groups
     wide = heads * group * HEAD_SIZE
     position = lax.axis_index("seq")
     valid = (position >= reach - jnp.arange(reach + 1)).astype(jnp.float32)
 
-    parts = []
-    for h in range(kv_heads):
-        cols = slice(h * HEAD_SIZE, (h + 1) * HEAD_SIZE)
-        parts += [key_matrix[:, cols], value_matrix[:, cols]]
-    weight = lax.all_gather(jnp.concatenate(parts, axis=1), "seq", axis=0, tiled=True)
+    weight = lax.all_gather(interleave(key_matrix, value_matrix), "seq", axis=0, tiled=True)
 
     raws, windows, outs, sums = [], [], [], []
     partial = None
@@ -325,26 +339,39 @@
     dlogits = (chosen * (probs - onehot) * (1.0 - (capped / softcap) ** 2)).astype(jnp.bfloat16)
     attended_grad = dot(dlogits, readout, NT).astype(jnp.bfloat16)
 
-    query_grads, grads = [], []
-    for n in range(groups):
+    query_grads, grads, pending = [], [], []
+    parts = min(BACKWARD_GROUPS, kv_heads)
+    some = kv_heads // parts
+    for n in range(parts):
+        if n >= 2:
+            attended_grad, pending[n - 2] = lax.optimization_barrier(
+                (attended_grad, pending[n - 2])
+            )
+        if n >= 3:
+            grads[n - 3] = post(*grads[n - 3])
+            attended_grad, grads[n - 3] = lax.optimization_barrier((attended_grad, grads[n - 3]))
+        at, inner = divmod(n * some, heads)
         query_grad, *pieces = attention_backward(
-            valid, queries, outs[n], attended_grad, sums[n], windows[n], n * heads, heads, group
+            valid, queries, outs[at], attended_grad, sums[at], windows[at], n * some, inner, some, group
         )
         query_grads.append(query_grad)
         total = pieces[0]
         for slot in range(1, reach):
             arrived = passed_along(total, "seq", -1).astype(jnp.float32)
             total = (arrived + pieces[slot]).astype(jnp.bfloat16)
-        grads.append(post(raws[n], passed_along(total, "seq", -1), pieces[reach]))
+        pending.append(total)
+        grads.append((raws[at], passed_along(total, "seq", -1), pieces[reach], inner))
+    grads = [post(*item) if isinstance(item, tuple) else item for item in grads]
 
     blocks = weight.shape[0] // COLUMNS
-    factors = [(weight, n) for n in range(groups)]
+    factors = [(weight, n) for n in range(parts)]
     if lax.axis_size("head") == 2:
         half = blocks // 2
         me = lax.axis_index("head")
         arrived = []
         done = 0
-        for size in (half // 3, half // 3, half - 2 * (half // 3)):
+        rest = (half - 1) // 2
+        for size in (1, rest, half - 1 - rest):
             term = product((1 - me) * half + done, size, grads, factors)
             arrived.append(swapped(term, "head"))
             done += size

time: 406 us -> 385 us (0.948); the launches traced: 399 us -> 383 us
  waiting for transfers between devices: 178 us -> 189 us
  local copies, waits for them, and re-layouts: 21.9 us -> 11.2 us
  Pallas kernels: 120 us -> 112 us
  starting transfers between devices: 46.7 us -> 39 us
    ppermute x16 -> x12, waiting for transfers between devices: 15.5 us -> 31.3 us  [passed_along(): lax.ppermute(value, axis, [(source, source + steps) for source in range(l...]
    unnamed x77 -> x44, local copies, waits for them, and re-layouts: 21.9 us -> 11.2 us
    pallas_call x4 -> x2, Pallas kernels: 28.9 us -> 20.8 us  [project(): pl.pallas_call(project_kernel, grid=(heads,), in_specs=[pl.BlockSpec((tok...]
    ppermute x16 -> x12, starting transfers between devices: 42.5 us -> 35 us  [passed_along(): lax.ppermute(value, axis, [(source, source + steps) for source in range(l...]
    ppermute x4, waiting for transfers between devices: 47 us -> 42.9 us  [swapped(): return lax.ppermute(value, axis, [(0, 1), (1, 0)])]
    pallas_call x4 -> x2, Pallas kernels: 19.1 us -> 17.6 us  [attention_forward(): pl.pallas_call(functools.partial(forward_kernel, reach, group), grid=(hea...]
  transfers between devices with their start and end apart: 21 -> 17, of which waited for: 11 -> 11; matrix products, arithmetic and copies ran while one was open for 2% -> 2% of each run, Pallas kernels for 23% -> 19%
where the time goes in v3:
time: 385 us; the launch traced here: 383 us
  waiting for transfers between devices  189 us (49%)
  Pallas kernels  112 us (29%)
  starting transfers between devices  39 us (10%)
  between operations  14.4 us (4%)
  other arithmetic  12.8 us (3%)
  local copies, waits for them, and re-layouts  11.2 us (3%)
  matrix products  4.64 us (1%)
    all_gather x1, waiting for transfers between devices, shards(): lax.all_gather(interleave(key_matrix, value_matrix), 'seq', axis=0, tiled...  115 us
    ppermute x4, waiting for transfers between devices, swapped(): return lax.ppermute(value, axis, [(0, 1), (1, 0)])  42.9 us
    pallas_call x4, Pallas kernels, attention_backward(): pl.pallas_call(functools.partial(backward_kernel, reach, group), grid=(he...  42.6 us
    ppermute x12, starting transfers between devices, passed_along(): lax.ppermute(value, axis, [(source, source + steps) for source in range(l...  35 us
    ppermute x12, waiting for transfers between devices, passed_along(): lax.ppermute(value, axis, [(source, source + steps) for source in range(l...  31.3 us
    pallas_call x4, Pallas kernels, product(): pl.pallas_call(functools.partial(product_kernel, count), grid_spec=pltpu....  24.8 us
    pallas_call x2, Pallas kernels, project(): pl.pallas_call(project_kernel, grid=(heads,), in_specs=[pl.BlockSpec((tok...  20.8 us
    pallas_call x2, Pallas kernels, attention_forward(): pl.pallas_call(functools.partial(forward_kernel, reach, group), grid=(hea...  17.6 us
  transfers between devices with their start and end apart: 17, of which 11 were waited for; matrix products, arithmetic and copies ran while one was open for 2% of the time, Pallas kernels for 19%

profile of v3, /device:TPU:13, one launch (start us, length us, event | category | flops | bytes accessed | tf_op | source)
XLA Modules:
  0.0 383.0 jit_solution(7140837791655184187)
XLA Ops:
  10.8 115.2 %all-gather.2.cloned.1.call-done.w_ref.refs_4_.refs_5_.refs_6_.refs_7_ = bf16[5376,2048]{1,0:T(8,128)(2,1)} async-done(((bf16[336,2048]{1,0:T(8,128)(2,1)}), bf16[5376,2048]{1,0:T(8,128)(2,1)}) %all-gather.2.cloned.1.call-update) | async-done | bytes 22020112 | tf_op jit(solution)/shard_map/all_gather | solution.py:309
  126.0 10.4 %shard_map.89 = (f32[512,1024]{1,0:T(8,128)S(1)}, bf16[512,1024]{1,0:T(8,128)(2,1)S(1)}) custom-call(bf16[512,5376]{1,0:T(8,128)(2,1)} %x_ref.3, bf16[5376,2048]{1,0:T(8,128)(2,1)} %all-gather.2.cloned.1.call-done.w_ref.refs_4_.refs_5_.refs_6_.refs_7_), custom_call_target="tpu_custom_call" | custom-call | flops 5637144576 | bytes 19660800 | tf_op jit(solution)/shard_map/pallas_call | solution.py:181
  137.8 3.5 collective-permute-start.2
  141.2 10.4 %shard_map.87 = (f32[512,1024]{1,0:T(8,128)S(1)}, bf16[512,1024]{1,0:T(8,128)(2,1)S(1)}) custom-call(bf16[512,5376]{1,0:T(8,128)(2,1)} %x_ref.3, bf16[5376,2048]{1,0:T(8,128)(2,1)} %all-gather.2.cloned.1.call-done.w_ref.refs_4_.refs_5_.refs_6_.refs_7_), custom_call_target="tpu_custom_call" | custom-call | flops 5637144576 | bytes 19660800 | tf_op jit(solution)/shard_map/pallas_call | solution.py:181
  154.9 3.5 collective-permute-start.3
  158.3 7.2 %collective-permute-done.refs_1_ = bf16[512,1024]{1,0:T(8,128)(2,1)} collective-permute-done((bf16[512,1024]{1,0:T(8,128)(2,1)S(1)}, bf16[512,1024]{1,0:T(8,128)(2,1)}, u32[]{:S(2)}, u32[]{:S(2)}) %collective-permute-start) | collective-permute-done | bytes 1048608 | tf_op jit(solution)/shard_map/ppermute | solution.py:30
  165.6 5.6 %collective-permute-start.1 = (bf16[512,1024]{1,0:T(8,128)(2,1)}, bf16[512,1024]{1,0:T(8,128)(2,1)}, u32[]{:S(2)}, u32[]{:S(2)}) collective-permute-start(bf16[512,1024]{1,0:T(8,128)(2,1)} %collective-permute-done.refs_1_), channel_id=1, source_target_pairs={{0,2},{2,4},{4,6},{6,8},{8,10},{10,12},{12,14},{14,16},{16,18},{18... | collective-permute-start | bytes 3145736 | tf_op jit(solution)/shard_map/ppermute | solution.py:30
  171.2 5.7 %collective-permute-done.3.refs_0_ = bf16[512,1024]{1,0:T(8,128)(2,1)} collective-permute-done((bf16[512,1024]{1,0:T(8,128)(2,1)}, bf16[512,1024]{1,0:T(8,128)(2,1)}, u32[]{:S(2)}, u32[]{:S(2)}) %collective-permute-start.3) | collective-permute-done | bytes 1048608 | tf_op jit(solution)/shard_map/ppermute | solution.py:30
  176.9 8.8 %shard_map.90 = (bf16[512,1024]{1,0:T(8,128)(2,1)S(1)}, f32[32,1024]{1,0:T(8,128)S(1)}) custom-call(f32[3]{0:T(128)S(1)} %compare_convert_fusion.valid_ref, bf16[512,2048]{1,0:T(8,128)(2,1)} %q_ref.11, bf16[512,1024]{1,0:T(8,128)(2,1)} %collective-permute-done.3.refs_0_, bf16[512,1024]{1,0:T(8,128)(2,1)} %collective-permute-done.2.refs_1_, ...), custom_call_target="tpu_custom_call" | custom-call | flops 5368709120 | bytes 5242880 | tf_op jit(solution)/shard_map/pallas_call | solution.py:248
  188.1 8.8 %shard_map.88 = (bf16[512,1024]{1,0:T(8,128)(2,1)S(1)}, f32[32,1024]{1,0:T(8,128)S(1)}) custom-call(f32[3]{0:T(128)S(1)} %compare_convert_fusion.valid_ref, bf16[512,2048]{1,0:T(8,128)(2,1)} %q_ref.11, bf16[512,1024]{1,0:T(8,128)(2,1)} %collective-permute-done.1.refs_0_, bf16[512,1024]{1,0:T(8,128)(2,1)} %collective-permute-done.refs_1_, ...), custom_call_target="tpu_custom_call" | custom-call | flops 5368709120 | bytes 5242880 | tf_op jit(solution)/shard_map/pallas_call | solution.py:248
  199.0 11.1 %collective-permute-done.4 = bf16[512,512]{0,1:T(8,128)(2,1)S(1)} collective-permute-done((bf16[512,512]{0,1:T(8,128)(2,1)S(1)}, bf16[512,512]{0,1:T(8,128)(2,1)S(1)}, u32[]{:S(2)}, u32[]{:S(2)}) %collective-permute-start.4) | collective-permute-done | bytes 524320 | tf_op jit(solution)/shard_map/ppermute | solution.py:34
  213.5 10.6 %shard_map.91 = (f32[512,512]{1,0:T(8,128)S(1)}, bf16[512,512]{1,0:T(8,128)(2,1)S(1)}, f32[512,512]{1,0:T(8,128)S(1)}, f32[512,512]{1,0:T(8,128)S(1)}) custom-call(f32[3]{0:T(128)S(1)} %compare_convert_fusion.valid_ref, bf16[512,2048]{1,0:T(8,128)(2,1)} %q_ref.11, bf16[512,1024]{1,0:T(8,128)(2,1)S(1)} %get-tuple-element.31.o_ref, ...), custom_call_target="tpu_custom_call" | custom-call | flops 5368709120 | bytes 6291456 | tf_op jit(solution)/shard_map/pallas_call | solution.py:274
  225.1 4.2 %collective-permute-start.5 = (bf16[512,512]{1,0:T(8,128)(2,1)S(1)}, bf16[512,512]{1,0:T(8,128)(2,1)S(1)}, u32[]{:S(2)}, u32[]{:S(2)}) collective-permute-start(bf16[512,512]{1,0:T(8,128)(2,1)S(1)} %get-tuple-element.37), channel_id=1, source_target_pairs={{2,0},{4,2},{6,4},{8,6},{10,8},{12,10},{14,12},{16,14},{18,16},{20... | collective-permute-start | bytes 1572872 | tf_op jit(solution)/shard_map/ppermute | solution.py:30
  229.3 10.7 %shard_map.92 = (f32[512,512]{1,0:T(8,128)S(1)}, bf16[512,512]{1,0:T(8,128)(2,1)S(1)}, f32[512,512]{1,0:T(8,128)S(1)}, f32[512,512]{1,0:T(8,128)S(1)}) custom-call(f32[3]{0:T(128)S(1)} %compare_convert_fusion.valid_ref, bf16[512,2048]{1,0:T(8,128)(2,1)} %q_ref.11, bf16[512,1024]{1,0:T(8,128)(2,1)S(1)} %get-tuple-element.31.o_ref, ...), custom_call_target="tpu_custom_call" | custom-call | flops 5368709120 | bytes 6291456 | tf_op jit(solution)/shard_map/pallas_call | solution.py:274
  244.4 7.0 %collective-permute-done.6 = bf16[512,512]{1,0:T(8,128)(2,1)S(1)} collective-permute-done((bf16[512,512]{1,0:T(8,128)(2,1)S(1)}, bf16[512,512]{1,0:T(8,128)(2,1)S(1)}, u32[]{:S(2)}, u32[]{:S(2)}) %collective-permute-start.6) | collective-permute-done | bytes 524320 | tf_op jit(solution)/shard_map/ppermute | solution.py:30
  252.4 10.6 %shard_map.93 = (f32[512,512]{1,0:T(8,128)S(1)}, bf16[512,512]{1,0:T(8,128)(2,1)S(1)}, f32[512,512]{1,0:T(8,128)S(1)}, f32[512,512]{1,0:T(8,128)S(1)}) custom-call(f32[3]{0:T(128)S(1)} %compare_convert_fusion.valid_ref, bf16[512,2048]{1,0:T(8,128)(2,1)} %q_ref.11, bf16[512,1024]{1,0:T(8,128)(2,1)S(1)} %get-tuple-element.33.o_ref, ...), custom_call_target="tpu_custom_call" | custom-call | flops 5368709120 | bytes 6291456 | tf_op jit(solution)/shard_map/pallas_call | solution.py:274
  266.9 10.6 %shard_map.95 = (f32[512,512]{1,0:T(8,128)S(1)}, bf16[512,512]{1,0:T(8,128)(2,1)S(1)}, f32[512,512]{1,0:T(8,128)S(1)}, f32[512,512]{1,0:T(8,128)S(1)}) custom-call(f32[3]{0:T(128)S(1)} %compare_convert_fusion.valid_ref, bf16[512,2048]{1,0:T(8,128)(2,1)} %q_ref.11, bf16[512,1024]{1,0:T(8,128)(2,1)S(1)} %get-tuple-element.33.o_ref, ...), custom_call_target="tpu_custom_call" | custom-call | flops 5368709120 | bytes 6291456 | tf_op jit(solution)/shard_map/pallas_call | solution.py:274
  282.4 4.0 %collective-permute-start.10 = (bf16[512,512]{1,0:T(8,128)(2,1)}, bf16[512,512]{1,0:T(8,128)(2,1)}, u32[]{:S(2)}, u32[]{:S(2)}) collective-permute-start(bf16[512,512]{1,0:T(8,128)(2,1)} %add_convert_fusion.1), channel_id=1, source_target_pairs={{2,0},{4,2},{6,4},{8,6},{10,8},{12,10},{14,12},{16,14},{18,16},{20... | collective-permute-start | bytes 1572872 | tf_op jit(solution)/shard_map/ppermute | solution.py:30
  307.5 5.4 %shard_map.101 = bf16[512,1152]{1,0:T(8,128)(2,1)S(1)} custom-call(s32[1]{0:T(128)} %bitcast.2.start_ref, bf16[512,512]{1,0:T(8,128)(2,1)S(1)} %shard_map.94.refs_0_, bf16[512,512]{1,0:T(8,128)(2,1)S(1)} %shard_map.96.refs_1_, bf16[512,512]{1,0:T(8,128)(2,1)S(1)} %shard_map.97.refs_2_, bf16[512,512]{1,0:T(8,128)(2,1)S(1)} %shard_map.98.refs_3_, ...), custom_call_target="tpu_custom_call" | custom-call | flops 2415919104 | bytes 7995392 | tf_op jit(solution)/shard_map/pallas_call | solution.py:209
  314.1 6.2 %shard_map.102 = bf16[512,1152]{1,0:T(8,128)(2,1)} custom-call(s32[1]{0:T(128)} %bitcast.3.start_ref, bf16[512,512]{1,0:T(8,128)(2,1)S(1)} %shard_map.94.refs_0_, bf16[512,512]{1,0:T(8,128)(2,1)S(1)} %shard_map.96.refs_1_, bf16[512,512]{1,0:T(8,128)(2,1)S(1)} %shard_map.97.refs_2_, bf16[512,512]{1,0:T(8,128)(2,1)S(1)} %shard_map.98.refs_3_, ...), custom_call_target="tpu_custom_call" | custom-call | flops 2415919104 | bytes 7995392 | tf_op jit(solution)/shard_map/pallas_call | solution.py:209
  320.6 4.6 %pad_maximum_fusion = f32[512,2048]{1,0:T(8,128)} fusion(f32[512,512]{1,0:T(8,128)} %copy-done.11, f32[512,512]{1,0:T(8,128)} %copy-done.10, f32[512,512]{1,0:T(8,128)} %copy-done.9, f32[512,512]{1,0:T(8,128)} %copy-done.8), kind=kLoop, calls=%fused_computation.1 | loop fusion | flops 3145728 | bytes 8388608 | tf_op jit(solution)/shard_map/concatenate | solution.py:384
  329.0 10.6 %shard_map.99 = bf16[512,2688]{1,0:T(8,128)(2,1)S(1)} custom-call(s32[1]{0:T(128)} %bitcast.start_ref, bf16[512,512]{1,0:T(8,128)(2,1)S(1)} %shard_map.94.refs_0_, bf16[512,512]{1,0:T(8,128)(2,1)S(1)} %shard_map.96.refs_1_, bf16[512,512]{1,0:T(8,128)(2,1)S(1)} %shard_map.97.refs_2_, bf16[512,512]{1,0:T(8,128)(2,1)S(1)} %shard_map.98.refs_3_, ...), custom_call_target="tpu_custom_call" | custom-call | flops 5637144576 | bytes 15859712 | tf_op jit(solution)/shard_map/pallas_call | solution.py:209
  339.7 31.8 %collective-permute-done.13 = bf16[512,384]{1,0:T(8,128)(2,1)S(1)} collective-permute-done((bf16[512,384]{1,0:T(8,128)(2,1)S(1)}, bf16[512,384]{1,0:T(8,128)(2,1)S(1)}, u32[]{:S(2)}, u32[]{:S(2)}) %collective-permute-start.13) | collective-permute-done | bytes 393248 | tf_op jit(solution)/shard_map/ppermute | solution.py:34
  371.5 4.7 %convert_add_fusion = f32[512,2688]{1,0:T(8,128)} fusion(bf16[512,2688]{1,0:T(8,128)(2,1)S(1)} %shard_map.99, bf16[512,1152]{1,0:T(8,128)(2,1)} %collective-permute-done.15, bf16[512,1152]{1,0:T(8,128)(2,1)} %collective-permute-done.14, bf16[512,384]{1,0:T(8,128)(2,1)S(1)} %collective-permute-done.13), kind=kLoop, calls=%fused_computation | loop fusion | flops 11010048 | bytes 11010048 | tf_op jit(solution)/shard_map/add | solution.py:379
  (84 shorter events, 57.4 us)
Async XLA Ops:
  7.2 118.8 %all-gather.2.cloned.1.call-start = ((), (), s32[]{:S(2)}) async-start(), calls=%async_computation | async-start | bytes 23396352 | tf_op jit(solution)/shard_map/all_gather | solution.py:309
  137.8 39.1 %copy-start.16 = (bf16[512,1024]{1,0:T(8,128)(2,1)}, bf16[512,1024]{1,0:T(8,128)(2,1)S(1)}, u32[]{:S(2)}) copy-start(bf16[512,1024]{1,0:T(8,128)(2,1)S(1)} %get-tuple-element.32.refs_2_) | copy-start | bytes 3145732
  137.8 17.1 %collective-permute-start.2 = (bf16[512,1024]{1,0:T(8,128)(2,1)S(1)}, bf16[512,1024]{1,0:T(8,128)(2,1)}, u32[]{:S(2)}, u32[]{:S(2)}) collective-permute-start(bf16[512,1024]{1,0:T(8,128)(2,1)S(1)} %get-tuple-element.32.refs_2_), channel_id=1, source_target_pairs={{0,2},{2,4},{4,6},{6,8},{8,10},{10,12},{12,14},{14,16},{16,18},{18... | collective-permute-start | bytes 3145736 | tf_op jit(solution)/shard_map/ppermute | solution.py:30
  151.7 13.9 %collective-permute-start = (bf16[512,1024]{1,0:T(8,128)(2,1)S(1)}, bf16[512,1024]{1,0:T(8,128)(2,1)}, u32[]{:S(2)}, u32[]{:S(2)}) collective-permute-start(bf16[512,1024]{1,0:T(8,128)(2,1)S(1)} %get-tuple-element.30.refs_2_), channel_id=1, source_target_pairs={{0,2},{2,4},{4,6},{6,8},{8,10},{10,12},{12,14},{14,16},{16,18},{18... | collective-permute-start | bytes 3145736 | tf_op jit(solution)/shard_map/ppermute | solution.py:30
  154.9 22.0 %collective-permute-start.3 = (bf16[512,1024]{1,0:T(8,128)(2,1)}, bf16[512,1024]{1,0:T(8,128)(2,1)}, u32[]{:S(2)}, u32[]{:S(2)}) collective-permute-start(bf16[512,1024]{1,0:T(8,128)(2,1)} %collective-permute-done.2.refs_1_), channel_id=1, source_target_pairs={{0,2},{2,4},{4,6},{6,8},{8,10},{10,12},{12,14},{14,16},{16,18},{18... | collective-permute-start | bytes 3145736 | tf_op jit(solution)/shard_map/ppermute | solution.py:30
  165.6 22.6 %collective-permute-start.1 = (bf16[512,1024]{1,0:T(8,128)(2,1)}, bf16[512,1024]{1,0:T(8,128)(2,1)}, u32[]{:S(2)}, u32[]{:S(2)}) collective-permute-start(bf16[512,1024]{1,0:T(8,128)(2,1)} %collective-permute-done.refs_1_), channel_id=1, source_target_pairs={{0,2},{2,4},{4,6},{6,8},{8,10},{10,12},{12,14},{14,16},{16,18},{18... | collective-permute-start | bytes 3145736 | tf_op jit(solution)/shard_map/ppermute | solution.py:30
  171.1 14.6 %copy-start.20 = (bf16[2048,512]{1,0:T(8,128)(2,1)S(1)}, bf16[2048,512]{1,0:T(8,128)(2,1)}, u32[]{:S(2)}) copy-start(bf16[2048,512]{1,0:T(8,128)(2,1)} %param.11) | copy-start | bytes 6291460
  196.9 13.4 %copy-start.21 = (s32[512]{0:T(512)S(1)}, s32[512]{0:T(512)}, u32[]{:S(2)}) copy-start(s32[512]{0:T(512)} %param.13) | copy-start | bytes 6148
  197.7 12.3 %collective-permute-start.4 = (bf16[512,512]{0,1:T(8,128)(2,1)S(1)}, bf16[512,512]{0,1:T(8,128)(2,1)S(1)}, u32[]{:S(2)}, u32[]{:S(2)}) collective-permute-start(bf16[512,512]{0,1:T(8,128)(2,1)S(1)} %fusion), channel_id=1, source_target_pairs={{0,1},{1,0},{2,3},{3,2},{4,5},{5,4},{6,7},{7,6},{8,9},{9,8},{10,11... | collective-permute-start | bytes 1572872 | tf_op jit(solution)/shard_map/ppermute | solution.py:34
  225.1 16.8 %collective-permute-start.5 = (bf16[512,512]{1,0:T(8,128)(2,1)S(1)}, bf16[512,512]{1,0:T(8,128)(2,1)S(1)}, u32[]{:S(2)}, u32[]{:S(2)}) collective-permute-start(bf16[512,512]{1,0:T(8,128)(2,1)S(1)} %get-tuple-element.37), channel_id=1, source_target_pairs={{2,0},{4,2},{6,4},{8,6},{10,8},{12,10},{14,12},{16,14},{18,16},{20... | collective-permute-start | bytes 1572872 | tf_op jit(solution)/shard_map/ppermute | solution.py:30
  240.0 12.4 %copy-start.2 = (f32[512,512]{1,0:T(8,128)}, f32[512,512]{1,0:T(8,128)S(1)}, u32[]{:S(2)}) copy-start(f32[512,512]{1,0:T(8,128)S(1)} %get-tuple-element.50.own_ref) | copy-start | bytes 3145732
  240.0 12.4 %copy-start.9 = (f32[512,512]{1,0:T(8,128)}, f32[512,512]{1,0:T(8,128)S(1)}, u32[]{:S(2)}) copy-start(f32[512,512]{1,0:T(8,128)S(1)} %get-tuple-element.36) | copy-start | bytes 3145732
  240.0 11.4 %collective-permute-start.6 = (bf16[512,512]{1,0:T(8,128)(2,1)S(1)}, bf16[512,512]{1,0:T(8,128)(2,1)S(1)}, u32[]{:S(2)}, u32[]{:S(2)}) collective-permute-start(bf16[512,512]{1,0:T(8,128)(2,1)S(1)} %get-tuple-element.42), channel_id=1, source_target_pairs={{2,0},{4,2},{6,4},{8,6},{10,8},{12,10},{14,12},{16,14},{18,16},{20... | collective-permute-start | bytes 1572872 | tf_op jit(solution)/shard_map/ppermute | solution.py:30
  242.1 24.1 %collective-permute-start.7 = (bf16[512,512]{1,0:T(8,128)(2,1)S(1)}, bf16[512,512]{1,0:T(8,128)(2,1)S(1)}, u32[]{:S(2)}, u32[]{:S(2)}) collective-permute-start(bf16[512,512]{1,0:T(8,128)(2,1)S(1)} %add_convert_fusion.3), channel_id=1, source_target_pairs={{2,0},{4,2},{6,4},{8,6},{10,8},{12,10},{14,12},{16,14},{18,16},{20... | collective-permute-start | bytes 1572872 | tf_op jit(solution)/shard_map/ppermute | solution.py:30
  264.0 17.5 %collective-permute-start.9 = (bf16[512,512]{1,0:T(8,128)(2,1)S(1)}, bf16[512,512]{1,0:T(8,128)(2,1)S(1)}, u32[]{:S(2)}, u32[]{:S(2)}) collective-permute-start(bf16[512,512]{1,0:T(8,128)(2,1)S(1)} %get-tuple-element.52), channel_id=1, source_target_pairs={{2,0},{4,2},{6,4},{8,6},{10,8},{12,10},{14,12},{16,14},{18,16},{20... | collective-permute-start | bytes 1572872 | tf_op jit(solution)/shard_map/ppermute | solution.py:30
  277.6 12.4 %copy-start.6 = (f32[512,512]{1,0:T(8,128)}, f32[512,512]{1,0:T(8,128)S(1)}, u32[]{:S(2)}) copy-start(f32[512,512]{1,0:T(8,128)S(1)} %get-tuple-element.57.own_ref) | copy-start | bytes 3145732
  277.6 12.4 %copy-start.11 = (f32[512,512]{1,0:T(8,128)}, f32[512,512]{1,0:T(8,128)S(1)}, u32[]{:S(2)}) copy-start(f32[512,512]{1,0:T(8,128)S(1)} %get-tuple-element.48) | copy-start | bytes 3145732
  277.6 11.4 %collective-permute-start.11 = (bf16[512,512]{1,0:T(8,128)(2,1)S(1)}, bf16[512,512]{1,0:T(8,128)(2,1)S(1)}, u32[]{:S(2)}, u32[]{:S(2)}) collective-permute-start(bf16[512,512]{1,0:T(8,128)(2,1)S(1)} %get-tuple-element.55), channel_id=1, source_target_pairs={{2,0},{4,2},{6,4},{8,6},{10,8},{12,10},{14,12},{16,14},{18,16},{20... | collective-permute-start | bytes 1572872 | tf_op jit(solution)/shard_map/ppermute | solution.py:30
  279.5 15.1 %collective-permute-start.8 = (bf16[512,512]{1,0:T(8,128)(2,1)}, bf16[512,512]{1,0:T(8,128)(2,1)S(1)}, u32[]{:S(2)}, u32[]{:S(2)}) collective-permute-start(bf16[512,512]{1,0:T(8,128)(2,1)} %add_convert_fusion.2), channel_id=1, source_target_pairs={{2,0},{4,2},{6,4},{8,6},{10,8},{12,10},{14,12},{16,14},{18,16},{20... | collective-permute-start | bytes 1572872 | tf_op jit(solution)/shard_map/ppermute | solution.py:30
  282.4 17.9 %collective-permute-start.10 = (bf16[512,512]{1,0:T(8,128)(2,1)}, bf16[512,512]{1,0:T(8,128)(2,1)}, u32[]{:S(2)}, u32[]{:S(2)}) collective-permute-start(bf16[512,512]{1,0:T(8,128)(2,1)} %add_convert_fusion.1), channel_id=1, source_target_pairs={{2,0},{4,2},{6,4},{8,6},{10,8},{12,10},{14,12},{16,14},{18,16},{20... | collective-permute-start | bytes 1572872 | tf_op jit(solution)/shard_map/ppermute | solution.py:30
  290.0 16.0 %collective-permute-start.12 = (bf16[512,512]{1,0:T(8,128)(2,1)}, bf16[512,512]{1,0:T(8,128)(2,1)}, u32[]{:S(2)}, u32[]{:S(2)}) collective-permute-start(bf16[512,512]{1,0:T(8,128)(2,1)} %add_convert_fusion), channel_id=1, source_target_pairs={{2,0},{4,2},{6,4},{8,6},{10,8},{12,10},{14,12},{16,14},{18,16},{20... | collective-permute-start | bytes 1572872 | tf_op jit(solution)/shard_map/ppermute | solution.py:30
  312.9 58.6 %collective-permute-start.14 = (bf16[512,1152]{1,0:T(8,128)(2,1)S(1)}, bf16[512,1152]{1,0:T(8,128)(2,1)}, u32[]{:S(2)}, u32[]{:S(2)}) collective-permute-start(bf16[512,1152]{1,0:T(8,128)(2,1)S(1)} %shard_map.101), channel_id=1, source_target_pairs={{0,1},{1,0},{2,3},{3,2},{4,5},{5,4},{6,7},{7,6},{8,9},{9,8},{10,11... | collective-permute-start | bytes 3538952 | tf_op jit(solution)/shard_map/ppermute | solution.py:34
  320.2 51.3 %collective-permute-start.15 = (bf16[512,1152]{1,0:T(8,128)(2,1)}, bf16[512,1152]{1,0:T(8,128)(2,1)}, u32[]{:S(2)}, u32[]{:S(2)}) collective-permute-start(bf16[512,1152]{1,0:T(8,128)(2,1)} %shard_map.102), channel_id=1, source_target_pairs={{0,1},{1,0},{2,3},{3,2},{4,5},{5,4},{6,7},{7,6},{8,9},{9,8},{10,11... | collective-permute-start | bytes 3538952 | tf_op jit(solution)/shard_map/ppermute | solution.py:34
  327.8 43.7 %collective-permute-start.13 = (bf16[512,384]{1,0:T(8,128)(2,1)S(1)}, bf16[512,384]{1,0:T(8,128)(2,1)S(1)}, u32[]{:S(2)}, u32[]{:S(2)}) collective-permute-start(bf16[512,384]{1,0:T(8,128)(2,1)S(1)} %shard_map.100), channel_id=1, source_target_pairs={{0,1},{1,0},{2,3},{3,2},{4,5},{5,4},{6,7},{7,6},{8,9},{9,8},{10,11... | collective-permute-start | bytes 1179656 | tf_op jit(solution)/shard_map/ppermute | solution.py:34
  (15 other events, 28.8 us)
Sparse Core Ops, SparseCore 0:
  10.9 115.0 all-gather.1
